TPU v7x, 256 devices: a whole 4x4x8 slice. The times are simulated.
256 devices in a mesh: train: 8 (over z_hi, y), tp: 16 (over z_lo, x), dp: 2 (over core).
Axes of the slice: x: 4, y: 4, z: 8 (z_hi: 2, z_lo: 4; z = z_hi * 4 + z_lo), core: 2. Of those that a mesh axis runs over, the one named last changes fastest.
Arguments:
- adapter_down_factor: bfloat16 [2, 2, 64, 8192], P(None, None, None, ('train', 'tp')), may hold values from -6 to 6
- adapter_up_factor: bfloat16 [2, 2, 1024, 64], P(None, None, ('train', 'tp')), may hold values from -0.75 to 0.75
- projection_weight: bfloat16 [2, 2, 1024, 8192], P(None, None, 'tp'), may hold values from -6 to 6
Outputs:
- merged: bfloat16 [2, 2, 1024, 8192], P(None, None, 'tp')
All inputs are finite; a program needn't handle non-finite values.
Results may differ from a plain program's by a relative error of at most 0.001.
Values may be sent and summed in bfloat16 or wider, within the bound.
No kernel may reach another device: no remote copies, remote signals or barrier semaphores. Data moves between devices by JAX's collectives and lax.ppermute only.
A program may use at most 64 MiB of HBM per device.

v0:
```python
import jax.numpy as jnp

adapter_scale = 2.0


def reference(adapter_down_factor, adapter_up_factor, projection_weight):
    weight_update = jnp.einsum(
        "eitd,eidh->eith",
        adapter_up_factor.astype(jnp.float32),
        adapter_down_factor.astype(jnp.float32),
    )
    return (projection_weight.astype(jnp.float32) + adapter_scale * weight_update).astype(
        jnp.bfloat16
    )


def solution(mesh):
    return reference
```

profile of v0, /device:TPU:1, one launch (start us, length us, event | category | flops | bytes accessed | tf_op | source)
XLA Modules:
  0.0 221.1 jit_solution(10289342602770817250)
XLA Ops:
  6.5 0.0 all-gather.5.cloned.1.call-start
  6.5 1.3 collective-permute-start
  7.9 0.9 copy
  8.8 49.6 %all-gather.1 = bf16[2,2,64,1024]{2,1,0,3:T(2,128)(2,1)S(1)} all-gather(bf16[2,2,64,64]{2,1,0,3:T(2,128)(2,1)S(1)} %copy), channel_id=3, replica_groups=[16,16]<=[8,16,2]T(0,2,1), dimensions={3}, use_global_device_ids=true | all-gather | bytes 557056 | tf_op args[0]
  58.4 1.3 dynamic-slice.2
  59.7 0.0 collective-permute-done
  59.7 34.7 %all-gather = bf16[2,2,64,64]{3,2,1,0:T(8,128)(2,1)S(1)} all-gather(bf16[2,2,8,64]{3,2,1,0:T(8,128)(2,1)S(1)} %collective-permute-done), channel_id=2, replica_groups=[32,8]<=[8,32]T(1,0), dimensions={2}, use_global_device_ids=true | all-gather | bytes 36864 | tf_op jit(solution)/call_exported
  94.4 2.9 %fusion.1 = bf16[2,2,64,1024]{3,2,1,0:T(8,128)(2,1)} fusion(bf16[2,2,64,64]{3,2,1,0:T(8,128)(2,1)S(1)} %all-gather, bf16[2,2,64,1024]{2,1,0,3:T(2,128)(2,1)S(1)} %all-gather.1, bf16[2,2,64,8192]{3,2,1,0:T(8,128)(2,1)} %param, s32[]{:T(128)} %bitcast), kind=kOutput, calls=%fused_computation.2 | convolution fusion | flops 34603008 | bytes 1605636 | tf_op jit(solution)/eitd,eidh->eith/dot_general | solution.py:7
  97.3 0.0 all-gather.5.cloned.1.call-update
  97.3 112.3 %all-gather.5.cloned.1.call-done = bf16[2,2,64,8192]{3,2,1,0:T(8,128)(2,1)} async-done(((bf16[2,2,64,1024]{3,2,1,0:T(8,128)(2,1)}), bf16[2,2,64,8192]{3,2,1,0:T(8,128)(2,1)}) %all-gather.5.cloned.1.call-update) | async-done | bytes 4194320 | tf_op jit(solution)/convert_element_type | solution.py:12
  209.6 4.6 %copy.5 = bf16[2,2,64,8192]{3,2,1,0:T(8,128)(2,1)} copy(bf16[2,2,64,8192]{3,2,1,0:T(8,128)(2,1)} %all-gather.5.cloned.1.call-done) | data formatting | bytes 8388608
Async XLA Ops:
  6.5 203.1 %all-gather.5.cloned.1.call-start = ((), (), s32[]{:S(2)}) async-start(), calls=%async_computation | async-start | bytes 4718592 | tf_op jit(solution)/convert_element_type | solution.py:12
  6.5 53.2 %collective-permute-start = (bf16[2,2,8,64]{3,2,1,0:T(8,128)(2,1)}, bf16[2,2,8,64]{3,2,1,0:T(8,128)(2,1)S(1)}, u32[]{:S(2)}, u32[]{:S(2)}) collective-permute-start(bf16[2,2,8,64]{3,2,1,0:T(8,128)(2,1)} %param.1), channel_id=1, source_target_pairs={{0,0},{1,1},{2,32},{3,33},{4,64},{5,65},{6,96},{7,97},{8,128},{9,1... | collective-permute-start | bytes 12296 | tf_op args[1]
Sparse Core Ops, SparseCore 0:
  97.4 112.1 all-gather.4
where the time goes:
time: 221 us
  waiting for transfers between devices  112 us (51%)
  blocking collectives  84.2 us (38%)
  between operations  13.4 us (6%)
  local copies, waits for them, and re-layouts  6.86 us (3%)
  matrix products  2.93 us (1%)
    convert_element_type x1, waiting for transfers between devices, reference(): (projection_weight.astype(jnp.float32) + adapter_scale * weight_update).a...  112 us
    unnamed x1, blocking collectives  49.6 us
    another operation x1, blocking collectives  34.7 us
    unnamed x2, local copies, waits for them, and re-layouts  5.57 us
  transfers between devices with their start and end apart: 2, of which 1 were waited for; matrix products, arithmetic and copies ran while one was open for 1% of the time, Pallas kernels for 0%

commit v1 on v0

v1 whole, which is shorter than its diff:
```python
import functools

import jax
import jax.numpy as jnp
from jax import lax
from jax.experimental import pallas as pl
from jax.experimental.pallas import tpu as pltpu
from jax.sharding import PartitionSpec as P


AXES = ("train", "tp", "dp")
NX, NY, NZ = 4, 4, 8
H = 64
UP = 8
ROWS = H + UP
CHUNK = 2048


def linear(x, y, z, c):
    return (((z >> 2) * NY + y) * 16 + (z & 3) * NX + x) * 2 + c


def coords():
    for x in range(NX):
        for y in range(NY):
            for z in range(NZ):
                for c in range(2):
                    yield x, y, z, c


def place(dx, dy, dz):
    return (
        ((dz >> 2) & 1) * 16
        + ((dz >> 1) & 1) * 8
        + ((dx >> 1) & 1) * 4
        + ((dy >> 1) & 1) * 2
        + (dz & 1)
    )


def colour_groups():
    groups = {}
    for x, y, z, c in coords():
        key = ((x ^ z) & 1, (y ^ z) & 1, c)
        groups.setdefault(key, [0] * 32)[place(x, y, z)] = linear(x, y, z, c)
    return list(groups.values())


def from_neighbour(axis):
    pairs = []
    for x, y, z, c in coords():
        q = [x, y, z]
        q[axis] += 1 if c == 0 else -1
        pairs.append((linear(x, y, z, c), linear(q[0] % NX, q[1] % NY, q[2] % NZ, c)))
    return pairs


def other_core():
    return [(linear(x, y, z, c), linear(x, y, z, 1 - c)) for x, y, z, c in coords()]


def merge_kernel(s_ref, a0, a1, a2, a3, w_ref, *rest):
    o_ref, u_ref = rest[-2:]
    lists = (a0, a1, a2, a3)
    mx, my, mz = s_ref[1], s_ref[2], s_ref[3]
    px = (mx ^ mz) & 1
    py = (my ^ mz) & 1

    @pl.when(pl.program_id(0) == 0)
    def _():
        b = (mz & 3) * NX + mx
        y = (b >> 1) & 3
        rows = []
        for j in range(8):
            x = j & 3
            z = (b >> 3) * 4 + (b & 1) * 2 + (j >> 2)
            rel = ((x ^ z ^ px) & 1) + 2 * ((y ^ z ^ py) & 1)
            k = place(x, y, z)
            row = lists[0][k][H:ROWS]
            for i in range(1, 4):
                row = jnp.where(rel == i, lists[i][k][H:ROWS], row)
            rows.append(row.astype(jnp.float32) * 2.0)
        u = jnp.concatenate(rows, axis=0)
        u = jnp.concatenate([u, u], axis=0)
        r = lax.broadcasted_iota(jnp.int32, u.shape, 0) // 64
        c = lax.broadcasted_iota(jnp.int32, u.shape, 1) // 64
        u_ref[...] = jnp.where(r == c, u, 0.0).astype(jnp.bfloat16)

    u = u_ref[...]
    zh = pl.program_id(0) >> 1
    y1 = pl.program_id(0) & 1
    for y0 in range(2):
        y = y1 * 2 + y0
        for z1 in range(2):
            for kind in range(2):
                z0 = py ^ (y0 ^ kind)
                z = zh * 4 + z1 * 2 + z0
                first = px ^ z0
                for xh in range(2):
                    ka = place(2 * xh + first, y, z)
                    kb = place(2 * xh + 1 - first, y, z)
                    a = lists[2 * kind][ka][:H]
                    b = lists[2 * kind + 1][kb][:H]
                    d = jnp.concatenate(
                        [jnp.where(first == 0, a, b), jnp.where(first == 0, b, a)], axis=0
                    )
                    delta = lax.dot_general(
                        u, d, (((1,), (1,)), ((), ())), preferred_element_type=jnp.float32
                    )
                    col = pl.multiple_of((y0 * 8 + z1 * 4 + z0 * 2 + xh) * 128, 128)
                    for p in range(2):
                        w = w_ref[0, p, :, pl.ds(col, 128)].astype(jnp.float32)
                        o_ref[0, p, :, pl.ds(col, 128)] = (
                            w + delta[p * 64 : p * 64 + 64]
                        ).astype(jnp.bfloat16)


def merge(scalars, lists, weight, out=None):
    block = pl.BlockSpec((1, 2, 64, CHUNK), lambda i, s: (s[0], 0, 0, i))
    whole = pl.BlockSpec((32, ROWS, 128), lambda i, s: (0, 0, 0), pipeline_mode=pl.Buffered(1))
    in_specs = [whole] * 4 + [block]
    args = [scalars, *lists, weight]
    aliases = {}
    if out is not None:
        in_specs.append(pl.BlockSpec(memory_space=pl.ANY))
        args.append(out)
        aliases = {6: 0}
    return pl.pallas_call(
        merge_kernel,
        grid_spec=pltpu.PrefetchScalarGridSpec(
            num_scalar_prefetch=1,
            grid=(weight.shape[-1] // CHUNK,),
            in_specs=in_specs,
            out_specs=block,
            scratch_shapes=[pltpu.VMEM((128, 128), jnp.bfloat16)],
        ),
        out_shape=jax.ShapeDtypeStruct(weight.shape, weight.dtype),
        input_output_aliases=aliases,
        compiler_params=pltpu.CompilerParams(vmem_limit_bytes=32 * 1024 * 1024),
        cost_estimate=pl.CostEstimate(
            flops=2 * 128 * 128 * 8192, bytes_accessed=6 * 1024 * 1024, transcendentals=0
        ),
    )(*args)


def solution(mesh):
    groups = colour_groups()

    def local(down, up, weight):
        core = lax.axis_index("dp")
        train = lax.axis_index("train")
        tp = lax.axis_index("tp")
        x = tp % NX
        y = train % NY
        z = (train // NY) * 4 + tp // NX

        d = lax.dynamic_index_in_dim(down, core, 0, keepdims=False).reshape(128, H).T
        u = lax.dynamic_index_in_dim(up, core, 0, keepdims=False)
        u = u.transpose(1, 0, 2).reshape(UP, 128)
        mine = jnp.concatenate([d, u], axis=0)

        many = jnp.broadcast_to(mine[None], (32, ROWS, 128))
        own = lax.all_to_all(many, AXES, 0, 0, axis_index_groups=groups, tiled=True)
        lists = [own] + [lax.ppermute(own, AXES, from_neighbour(a)) for a in range(3)]
        swapped = [lax.ppermute(a, AXES, other_core()) for a in lists]

        here = jnp.stack([core, x, y, z]).astype(jnp.int32)
        there = jnp.stack([1 - core, x, y, z]).astype(jnp.int32)
        out = merge(here, lists, weight)
        return merge(there, swapped, weight, out)

    spec = P(None, None, "tp", None)
    return jax.shard_map(
        local,
        mesh=mesh,
        in_specs=(
            P(None, None, None, ("train", "tp")),
            P(None, None, ("train", "tp"), None),
            spec,
        ),
        out_specs=spec,
        check_vma=False,
    )
```

time: 221 us -> 61.4 us (0.28)
  waiting for transfers between devices: 112 us -> 3.72 us
  blocking collectives: 84.2 us -> 32.2 us
  between operations: 13.4 us -> 0.06 us
  starting transfers between devices: 1.34 us -> 12.5 us
  Pallas kernels: 0 us -> 9.45 us
  local copies, waits for them, and re-layouts: 6.86 us -> 3.2 us
  matrix products: 2.93 us -> 0 us
    convert_element_type x1 -> x0, waiting for transfers between devices: 112 us -> none  [reference(): (projection_weight.astype(jnp.float32) + adapter_scale * weight_update).a...]
    unnamed x1 -> x0, blocking collectives: 49.6 us -> none
    another operation x1 -> x0, blocking collectives: 34.7 us -> none
    all_to_all x0 -> x1, blocking collectives: none -> 32.2 us  [local(): own = lax.all_to_all(many, AXES, 0, 0, axis_index_groups=groups, tiled=True)]
    ppermute x0 -> x7, starting transfers between devices: none -> 12.5 us  [the longest x4 8.57 us: local(): swapped = [lax.ppermute(a, AXES, other_core()) for a in lists]]
    pallas_call x0 -> x2, Pallas kernels: none -> 9.45 us  [merge(): pl.pallas_call(merge_kernel, grid_spec=pltpu.PrefetchScalarGridSpec(num_s...]
    ppermute x0 -> x7, waiting for transfers between devices: none -> 3.72 us  [the longest x3 3.71 us: local(): lax.ppermute(own, AXES, from_neighbour(a))]
    unnamed x2 -> x6, local copies, waits for them, and re-layouts: 5.57 us -> 2.22 us
  transfers between devices with their start and end apart: 2 -> 7, of which waited for: 1 -> 1; matrix products, arithmetic and copies ran while one was open for 1% -> 0% of each run, Pallas kernels for 0% -> 9%
where the time goes in v1:
time: 61.4 us; the launch traced here: 61.2 us
  blocking collectives  32.2 us (52%)
  starting transfers between devices  12.5 us (20%)
  Pallas kernels  9.45 us (15%)
  waiting for transfers between devices  3.72 us (6%)
  local copies, waits for them, and re-layouts  3.2 us (5%)
    all_to_all x1, blocking collectives, local(): own = lax.all_to_all(many, AXES, 0, 0, axis_index_groups=groups, tiled=True)  32.2 us
    pallas_call x2, Pallas kernels, merge(): pl.pallas_call(merge_kernel, grid_spec=pltpu.PrefetchScalarGridSpec(num_s...  9.45 us
    ppermute x4, starting transfers between devices, local(): swapped = [lax.ppermute(a, AXES, other_core()) for a in lists]  8.57 us
    ppermute x3, starting transfers between devices, local(): lax.ppermute(own, AXES, from_neighbour(a))  3.91 us
    ppermute x3, waiting for transfers between devices, local(): lax.ppermute(own, AXES, from_neighbour(a))  3.71 us
    unnamed x6, local copies, waits for them, and re-layouts  2.22 us
  transfers between devices with their start and end apart: 7, of which 1 were waited for; matrix products, arithmetic and copies ran while one was open for 0% of the time, Pallas kernels for 9%

profile of v1, /device:TPU:1, one launch (start us, length us, event | category | flops | bytes accessed | tf_op | source)
XLA Modules:
  0.0 61.2 jit_solution(14675332536533037093)
XLA Ops:
  0.0 0.0 copy-start
  0.0 0.7 %dynamic-slice_bitcast_fusion = bf16[8,2,64]{2,0,1:T(8,128)(2,1)S(1)} fusion(bf16[2,2,8,64]{3,2,1,0:T(8,128)(2,1)} %param.4, s32[]{:T(128)S(6)} %select_n.28), kind=kLoop, calls=%fused_computation.1 | loop fusion | bytes 4100 | tf_op jit(solution)/shard_map/transpose | solution.py:159
  0.7 0.1 reshape.9
  0.8 0.0 copy-done
  0.8 0.1 copy.7
  1.0 0.1 broadcast_in_dim.2
  1.0 32.2 %all_to_all.5.a0 = bf16[32,72,128]{2,1,0:T(8,128)(2,1)S(1)} all-to-all(bf16[32,72,128]{2,1,0:T(8,128)(2,1)S(1)} %broadcast_in_dim.2), channel_id=1, replica_groups={{0,42,64,106,4,46,68,110,16,58,80,122,20,62,84,126,128,170,192,234,132,..., dimensions={0} | all-to-all | bytes 1179648 | tf_op jit(solution)/shard_map/all_to_all | solution.py:163
  33.3 2.7 %collective-permute-start.5 = (bf16[32,72,128]{2,1,0:T(8,128)(2,1)S(1)}, bf16[32,72,128]{2,1,0:T(8,128)(2,1)}, u32[]{:S(2)}, u32[]{:S(2)}) collective-permute-start(bf16[32,72,128]{2,1,0:T(8,128)(2,1)S(1)} %all_to_all.5.a0), channel_id=1, source_target_pairs={{0,8},{1,153},{8,16},{9,1},{16,24},{17,9},{24,128},{25,17},{128,13... | collective-permute-start | bytes 1769480 | tf_op jit(solution)/shard_map/ppermute | solution.py:164
  35.9 0.3 collective-permute-start.3
  36.3 0.9 %collective-permute-start.1 = (bf16[32,72,128]{2,1,0:T(8,128)(2,1)S(1)}, bf16[32,72,128]{2,1,0:T(8,128)(2,1)}, u32[]{:S(2)}, u32[]{:S(2)}) collective-permute-start(bf16[32,72,128]{2,1,0:T(8,128)(2,1)S(1)} %all_to_all.5.a0), channel_id=1, source_target_pairs={{0,2},{1,7},{8,10},{9,15},{16,18},{17,23},{24,26},{25,31},{128,130... | collective-permute-start | bytes 1769480 | tf_op jit(solution)/shard_map/ppermute | solution.py:164
  37.2 1.9 %collective-permute-start = (bf16[32,72,128]{2,1,0:T(8,128)(2,1)S(1)}, bf16[32,72,128]{2,1,0:T(8,128)(2,1)S(1)}, u32[]{:S(2)}, u32[]{:S(2)}) collective-permute-start(bf16[32,72,128]{2,1,0:T(8,128)(2,1)S(1)} %all_to_all.5.a0), channel_id=1, source_target_pairs={{0,1},{1,0},{8,9},{9,8},{16,17},{17,16},{24,25},{25,24},{128,129},... | collective-permute-start | bytes 1769480 | tf_op jit(solution)/shard_map/ppermute | solution.py:165
  39.0 3.7 %collective-permute-done.5.a3 = bf16[32,72,128]{2,1,0:T(8,128)(2,1)} collective-permute-done((bf16[32,72,128]{2,1,0:T(8,128)(2,1)S(1)}, bf16[32,72,128]{2,1,0:T(8,128)(2,1)}, u32[]{:S(2)}, u32[]{:S(2)}) %collective-permute-start.5) | collective-permute-done | bytes 589856 | tf_op jit(solution)/shard_map/ppermute | solution.py:164
  42.7 5.8 %collective-permute-start.6 = (bf16[32,72,128]{2,1,0:T(8,128)(2,1)}, bf16[32,72,128]{2,1,0:T(8,128)(2,1)S(1)}, u32[]{:S(2)}, u32[]{:S(2)}) collective-permute-start(bf16[32,72,128]{2,1,0:T(8,128)(2,1)} %collective-permute-done.5.a3), channel_id=1, source_target_pairs={{0,1},{1,0},{8,9},{9,8},{16,17},{17,16},{24,25},{25,24},{128,129},... | collective-permute-start | bytes 1769480 | tf_op jit(solution)/shard_map/ppermute | solution.py:165
  48.6 0.0 collective-permute-done.3.a2
  48.6 0.7 %collective-permute-start.4 = (bf16[32,72,128]{2,1,0:T(8,128)(2,1)}, bf16[32,72,128]{2,1,0:T(8,128)(2,1)S(1)}, u32[]{:S(2)}, u32[]{:S(2)}) collective-permute-start(bf16[32,72,128]{2,1,0:T(8,128)(2,1)} %collective-permute-done.3.a2), channel_id=1, source_target_pairs={{0,1},{1,0},{8,9},{9,8},{16,17},{17,16},{24,25},{25,24},{128,129},... | collective-permute-start | bytes 1769480 | tf_op jit(solution)/shard_map/ppermute | solution.py:165
  49.2 0.0 collective-permute-done.1.a1
  49.2 0.2 collective-permute-start.2
  49.5 0.1 add_add_fusion
  49.5 0.0 copy-start.1
  49.5 2.2 %copy-done.1 = bf16[2,2,64,8192]{3,2,1,0:T(8,128)(2,1)S(1)} copy-done((bf16[2,2,64,8192]{3,2,1,0:T(8,128)(2,1)S(1)}, bf16[2,2,64,8192]{3,2,1,0:T(8,128)(2,1)}, u32[]{:S(2)}) %copy-start.1) | copy-done | bytes 4194328
  51.7 0.0 copy-start.2
  51.7 5.6 %shard_map.37.rest_0_ = bf16[2,2,64,8192]{3,2,1,0:T(8,128)(2,1)} custom-call(s32[4]{0:T(128)S(1)} %get-tuple-element.6.s_ref, bf16[32,72,128]{2,1,0:T(8,128)(2,1)S(1)} %all_to_all.5.a0, bf16[32,72,128]{2,1,0:T(8,128)(2,1)} %collective-permute-done.1.a1, bf16[32,72,128]{2,1,0:T(8,128)(2,1)} %collective-permute-done.3.a2, ...), custom_call_target="tpu_custom_call" | custom-call | flops 268435456 | bytes 6291456 | tf_op jit(solution)/shard_map/pallas_call | solution.py:128
  57.3 0.0 collective-permute-done.a0
  57.3 0.0 collective-permute-done.6.a3
  57.3 0.0 collective-permute-done.4.a2
  57.3 0.0 collective-permute-done.2.a1
  57.3 0.0 copy-done.2
  57.3 3.9 %shard_map.38 = bf16[2,2,64,8192]{3,2,1,0:T(8,128)(2,1)} custom-call(s32[4]{0:T(128)S(1)} %get-tuple-element.5.s_ref, bf16[32,72,128]{2,1,0:T(8,128)(2,1)S(1)} %collective-permute-done.a0, bf16[32,72,128]{2,1,0:T(8,128)(2,1)S(1)} %collective-permute-done.2.a1, bf16[32,72,128]{2,1,0:T(8,128)(2,1)S(1)} %collective-permute-done.4.a2, ...), custom_call_target="tpu_custom_call", output_to_operand_aliasing={{}: (6, {})} | custom-call | flops 268435456 | bytes 6291456 | tf_op jit(solution)/shard_map/pallas_call | solution.py:128
  (3 shorter events, 0.0 us)
Async XLA Ops:
  0.0 0.8 %copy-start = (bf16[2,2,64,64]{3,2,1,0:T(8,128)(2,1)S(1)}, bf16[2,2,64,64]{3,2,1,0:T(8,128)(2,1)}, u32[]{:S(2)}) copy-start(bf16[2,2,64,64]{3,2,1,0:T(8,128)(2,1)} %param.3) | copy-start | bytes 98308
  33.3 9.5 %collective-permute-start.5 = (bf16[32,72,128]{2,1,0:T(8,128)(2,1)S(1)}, bf16[32,72,128]{2,1,0:T(8,128)(2,1)}, u32[]{:S(2)}, u32[]{:S(2)}) collective-permute-start(bf16[32,72,128]{2,1,0:T(8,128)(2,1)S(1)} %all_to_all.5.a0), channel_id=1, source_target_pairs={{0,8},{1,153},{8,16},{9,1},{16,24},{17,9},{24,128},{25,17},{128,13... | collective-permute-start | bytes 1769480 | tf_op jit(solution)/shard_map/ppermute | solution.py:164
  35.9 12.6 %collective-permute-start.3 = (bf16[32,72,128]{2,1,0:T(8,128)(2,1)S(1)}, bf16[32,72,128]{2,1,0:T(8,128)(2,1)}, u32[]{:S(2)}, u32[]{:S(2)}) collective-permute-start(bf16[32,72,128]{2,1,0:T(8,128)(2,1)S(1)} %all_to_all.5.a0), channel_id=1, source_target_pairs={{0,32},{1,97},{8,40},{9,105},{16,48},{17,113},{24,56},{25,121},{12... | collective-permute-start | bytes 1769480 | tf_op jit(solution)/shard_map/ppermute | solution.py:164
  36.3 13.0 %collective-permute-start.1 = (bf16[32,72,128]{2,1,0:T(8,128)(2,1)S(1)}, bf16[32,72,128]{2,1,0:T(8,128)(2,1)}, u32[]{:S(2)}, u32[]{:S(2)}) collective-permute-start(bf16[32,72,128]{2,1,0:T(8,128)(2,1)S(1)} %all_to_all.5.a0), channel_id=1, source_target_pairs={{0,2},{1,7},{8,10},{9,15},{16,18},{17,23},{24,26},{25,31},{128,130... | collective-permute-start | bytes 1769480 | tf_op jit(solution)/shard_map/ppermute | solution.py:164
  37.2 20.1 %collective-permute-start = (bf16[32,72,128]{2,1,0:T(8,128)(2,1)S(1)}, bf16[32,72,128]{2,1,0:T(8,128)(2,1)S(1)}, u32[]{:S(2)}, u32[]{:S(2)}) collective-permute-start(bf16[32,72,128]{2,1,0:T(8,128)(2,1)S(1)} %all_to_all.5.a0), channel_id=1, source_target_pairs={{0,1},{1,0},{8,9},{9,8},{16,17},{17,16},{24,25},{25,24},{128,129},... | collective-permute-start | bytes 1769480 | tf_op jit(solution)/shard_map/ppermute | solution.py:165
  42.7 14.5 %collective-permute-start.6 = (bf16[32,72,128]{2,1,0:T(8,128)(2,1)}, bf16[32,72,128]{2,1,0:T(8,128)(2,1)S(1)}, u32[]{:S(2)}, u32[]{:S(2)}) collective-permute-start(bf16[32,72,128]{2,1,0:T(8,128)(2,1)} %collective-permute-done.5.a3), channel_id=1, source_target_pairs={{0,1},{1,0},{8,9},{9,8},{16,17},{17,16},{24,25},{25,24},{128,129},... | collective-permute-start | bytes 1769480 | tf_op jit(solution)/shard_map/ppermute | solution.py:165
  48.6 8.7 %collective-permute-start.4 = (bf16[32,72,128]{2,1,0:T(8,128)(2,1)}, bf16[32,72,128]{2,1,0:T(8,128)(2,1)S(1)}, u32[]{:S(2)}, u32[]{:S(2)}) collective-permute-start(bf16[32,72,128]{2,1,0:T(8,128)(2,1)} %collective-permute-done.3.a2), channel_id=1, source_target_pairs={{0,1},{1,0},{8,9},{9,8},{16,17},{17,16},{24,25},{25,24},{128,129},... | collective-permute-start | bytes 1769480 | tf_op jit(solution)/shard_map/ppermute | solution.py:165
  49.2 8.1 %collective-permute-start.2 = (bf16[32,72,128]{2,1,0:T(8,128)(2,1)}, bf16[32,72,128]{2,1,0:T(8,128)(2,1)S(1)}, u32[]{:S(2)}, u32[]{:S(2)}) collective-permute-start(bf16[32,72,128]{2,1,0:T(8,128)(2,1)} %collective-permute-done.1.a1), channel_id=1, source_target_pairs={{0,1},{1,0},{8,9},{9,8},{16,17},{17,16},{24,25},{25,24},{128,129},... | collective-permute-start | bytes 1769480 | tf_op jit(solution)/shard_map/ppermute | solution.py:165
  49.5 2.2 %copy-start.1 = (bf16[2,2,64,8192]{3,2,1,0:T(8,128)(2,1)S(1)}, bf16[2,2,64,8192]{3,2,1,0:T(8,128)(2,1)}, u32[]{:S(2)}) copy-start(bf16[2,2,64,8192]{3,2,1,0:T(8,128)(2,1)} %w_ref.3) | copy-start | bytes 12582916
  51.7 5.6 %copy-start.2 = (bf16[2,2,64,8192]{3,2,1,0:T(8,128)(2,1)S(1)}, bf16[2,2,64,8192]{3,2,1,0:T(8,128)(2,1)}, u32[]{:S(2)}) copy-start(bf16[2,2,64,8192]{3,2,1,0:T(8,128)(2,1)} %w_ref.3) | copy-start | bytes 12582916

commit v2 on v1

v2 whole, which is shorter than its diff:
```python
import jax
import jax.numpy as jnp
from jax import lax
from jax.experimental import pallas as pl
from jax.experimental.pallas import tpu as pltpu
from jax.sharding import PartitionSpec as P


AXES = ("train", "tp", "dp")
NX, NY, NZ = 4, 4, 8
H = 64
UP = 8
ROWS = H + UP
CHUNK = 2048
CHUNKS = 4
VMEM_LIMIT = 16 * 1024 * 1024


def linear(x, y, z, c):
    return (((z >> 2) * NY + y) * 16 + (z & 3) * NX + x) * 2 + c


def coords():
    for x in range(NX):
        for y in range(NY):
            for z in range(NZ):
                for c in range(2):
                    yield x, y, z, c


def place(dx, dy, dz):
    return (
        ((dz >> 2) & 1) * 16
        + ((dz >> 1) & 1) * 8
        + ((dx >> 1) & 1) * 4
        + ((dy >> 1) & 1) * 2
        + (dz & 1)
    )


def colour_groups():
    groups = {}
    for x, y, z, c in coords():
        key = ((x ^ z) & 1, (y ^ z) & 1, c)
        groups.setdefault(key, [0] * 32)[place(x, y, z)] = linear(x, y, z, c)
    return list(groups.values())


def from_neighbour(axis):
    pairs = []
    for x, y, z, c in coords():
        q = [x, y, z]
        q[axis] += 1 if c == 0 else -1
        pairs.append((linear(x, y, z, c), linear(q[0] % NX, q[1] % NY, q[2] % NZ, c)))
    return pairs


def other_core():
    return [(linear(x, y, z, c), linear(x, y, z, 1 - c)) for x, y, z, c in coords()]


def merge_kernel(s_ref, a0, a1, a2, a3, w_ref, *rest):
    o_ref, buf, u_ref, load_sem, store_sem = rest[-5:]
    lists = (a0, a1, a2, a3)
    layer, mx, my, mz = s_ref[0], s_ref[1], s_ref[2], s_ref[3]
    px = (mx ^ mz) & 1
    py = (my ^ mz) & 1

    def part(ref, i):
        return ref.at[layer, :, :, pl.ds(i * CHUNK, CHUNK)]

    def load(i):
        return pltpu.make_async_copy(part(w_ref, i), buf.at[i], load_sem.at[i])

    def store(i):
        return pltpu.make_async_copy(buf.at[i], part(o_ref, i), store_sem.at[i])

    for i in range(CHUNKS):
        load(i).start()

    b = (mz & 3) * NX + mx
    y = (b >> 1) & 3
    rows = []
    for j in range(8):
        x = j & 3
        z = (b >> 3) * 4 + (b & 1) * 2 + (j >> 2)
        rel = ((x ^ z ^ px) & 1) + 2 * ((y ^ z ^ py) & 1)
        k = place(x, y, z)
        row = lists[0][k, H:ROWS]
        for i in range(1, 4):
            row = jnp.where(rel == i, lists[i][k, H:ROWS], row)
        rows.append(row.astype(jnp.float32) * 2.0)
    u = jnp.concatenate(rows, axis=0)
    u = jnp.concatenate([u, u], axis=0)
    r = lax.broadcasted_iota(jnp.int32, u.shape, 0) // 64
    c = lax.broadcasted_iota(jnp.int32, u.shape, 1) // 64
    u_ref[...] = jnp.where(r == c, u, 0.0).astype(jnp.bfloat16)

    for i in range(CHUNKS):
        u = u_ref[...]
        zh, y1 = i >> 1, i & 1
        load(i).wait()
        for y0 in range(2):
            y = y1 * 2 + y0
            for z1 in range(2):
                for kind in range(2):
                    z0 = py ^ (y0 ^ kind)
                    z = zh * 4 + z1 * 2 + z0
                    first = px ^ z0
                    parts = []
                    for xh in range(2):
                        k = place(2 * xh, y, z)
                        even = lists[2 * kind][k, :H]
                        odd = lists[2 * kind + 1][k, :H]
                        parts.append(jnp.where(first == 0, even, odd))
                        parts.append(jnp.where(first == 0, odd, even))
                    delta = lax.dot_general(
                        u,
                        jnp.concatenate(parts, axis=0),
                        (((1,), (1,)), ((), ())),
                        preferred_element_type=jnp.float32,
                    )
                    at = pl.multiple_of((y0 * 4 + z1 * 2 + z0) * 256, 256)
                    for p in range(2):
                        w = buf[i, p, :, pl.ds(at, 256)].astype(jnp.float32)
                        buf[i, p, :, pl.ds(at, 256)] = (
                            w + delta[p * 64 : p * 64 + 64]
                        ).astype(jnp.bfloat16)
        store(i).start()
    for i in range(CHUNKS):
        store(i).wait()


def merge(scalars, lists, weight, out=None):
    inside = pl.BlockSpec(memory_space=pltpu.VMEM)
    outside = pl.BlockSpec(memory_space=pl.ANY)
    in_specs = [pl.BlockSpec(memory_space=pltpu.SMEM)] + [inside] * 4 + [outside]
    args = [scalars, *lists, pltpu.with_memory_space_constraint(weight, pltpu.HBM)]
    aliases = {}
    if out is not None:
        in_specs.append(outside)
        args.append(out)
        aliases = {6: 0}
    return pl.pallas_call(
        merge_kernel,
        in_specs=in_specs,
        out_specs=outside,
        out_shape=jax.ShapeDtypeStruct(weight.shape, weight.dtype),
        scratch_shapes=[
            pltpu.VMEM((CHUNKS, 2, 64, CHUNK), jnp.bfloat16),
            pltpu.VMEM((128, 128), jnp.bfloat16),
            pltpu.SemaphoreType.DMA((CHUNKS,)),
            pltpu.SemaphoreType.DMA((CHUNKS,)),
        ],
        input_output_aliases=aliases,
        compiler_params=pltpu.CompilerParams(vmem_limit_bytes=VMEM_LIMIT),
        cost_estimate=pl.CostEstimate(
            flops=2 * 128 * 128 * 8192, bytes_accessed=6 * 1024 * 1024, transcendentals=0
        ),
    )(*args)


def solution(mesh):
    groups = colour_groups()

    def local(down, up, weight):
        core = lax.axis_index("dp")
        train = lax.axis_index("train")
        tp = lax.axis_index("tp")
        x = tp % NX
        y = train % NY
        z = (train // NY) * 4 + tp // NX

        d = lax.dynamic_index_in_dim(down, core, 0, keepdims=False).reshape(128, H).T
        u = lax.dynamic_index_in_dim(up, core, 0, keepdims=False)
        u = u.transpose(1, 0, 2).reshape(UP, 128)
        mine = jnp.concatenate([d, u], axis=0)

        many = jnp.broadcast_to(mine[None], (32, ROWS, 128))
        own = lax.all_to_all(many, AXES, 0, 0, axis_index_groups=groups, tiled=True)
        lists = [own] + [lax.ppermute(own, AXES, from_neighbour(a)) for a in range(3)]
        swapped = [lax.ppermute(a, AXES, other_core()) for a in lists]

        here = jnp.stack([core, x, y, z]).astype(jnp.int32)
        there = jnp.stack([1 - core, x, y, z]).astype(jnp.int32)
        out = merge(here, lists, weight)
        return merge(there, swapped, weight, out)

    spec = P(None, None, "tp", None)
    return jax.shard_map(
        local,
        mesh=mesh,
        in_specs=(
            P(None, None, None, ("train", "tp")),
            P(None, None, ("train", "tp"), None),
            spec,
        ),
        out_specs=spec,
        check_vma=False,
    )
```

time: 61.4 us -> 58.3 us (0.950)
  local copies, waits for them, and re-layouts: 3.2 us -> 1.01 us
  Pallas kernels: 9.45 us -> 8.54 us
    unnamed x6 -> x2, local copies, waits for them, and re-layouts: 2.22 us -> 0.02 us
    pallas_call x2, Pallas kernels: 9.45 us -> 8.54 us  [merge(): pl.pallas_call(merge_kernel, in_specs=in_specs, out_specs=outside, out_sh...]
  transfers between devices with their start and end apart: 7 -> 7, of which waited for: 1 -> 1; matrix products, arithmetic and copies ran while one was open for 0% -> 0% of each run, Pallas kernels for 9% -> 8%
where the time goes in v2:
time: 58.3 us; the launch traced here: 58.1 us
  blocking collectives  32.2 us (55%)
  starting transfers between devices  12.5 us (21%)
  Pallas kernels  8.54 us (15%)
  waiting for transfers between devices  3.72 us (6%)
  local copies, waits for them, and re-layouts  1.01 us (2%)
    all_to_all x1, blocking collectives, local(): own = lax.all_to_all(many, AXES, 0, 0, axis_index_groups=groups, tiled=True)  32.2 us
    ppermute x4, starting transfers between devices, local(): swapped = [lax.ppermute(a, AXES, other_core()) for a in lists]  8.57 us
    pallas_call x2, Pallas kernels, merge(): pl.pallas_call(merge_kernel, in_specs=in_specs, out_specs=outside, out_sh...  8.54 us
    ppermute x3, starting transfers between devices, local(): lax.ppermute(own, AXES, from_neighbour(a))  3.91 us
    ppermute x3, waiting for transfers between devices, local(): lax.ppermute(own, AXES, from_neighbour(a))  3.71 us
  transfers between devices with their start and end apart: 7, of which 1 were waited for; matrix products, arithmetic and copies ran while one was open for 0% of the time, Pallas kernels for 8%

profile of v2, /device:TPU:1, one launch (start us, length us, event | category | flops | bytes accessed | tf_op | source)
XLA Modules:
  0.0 58.1 jit_solution(8324974842881531459)
XLA Ops:
  0.0 0.0 copy-start
  0.0 0.7 %dynamic-slice_bitcast_fusion = bf16[8,2,64]{2,0,1:T(8,128)(2,1)S(1)} fusion(bf16[2,2,8,64]{3,2,1,0:T(8,128)(2,1)} %param.4, s32[]{:T(128)S(6)} %select_n.28), kind=kLoop, calls=%fused_computation.1 | loop fusion | bytes 4100 | tf_op jit(solution)/shard_map/transpose | solution.py:176
  0.7 0.1 reshape.9
  0.8 0.0 copy-done
  0.8 0.1 copy.7
  1.0 0.1 broadcast_in_dim.2
  1.0 32.2 %all_to_all.5.a0 = bf16[32,72,128]{2,1,0:T(8,128)(2,1)S(1)} all-to-all(bf16[32,72,128]{2,1,0:T(8,128)(2,1)S(1)} %broadcast_in_dim.2), channel_id=1, replica_groups={{0,42,64,106,4,46,68,110,16,58,80,122,20,62,84,126,128,170,192,234,132,..., dimensions={0} | all-to-all | bytes 1179648 | tf_op jit(solution)/shard_map/all_to_all | solution.py:180
  33.3 2.7 %collective-permute-start.5 = (bf16[32,72,128]{2,1,0:T(8,128)(2,1)S(1)}, bf16[32,72,128]{2,1,0:T(8,128)(2,1)}, u32[]{:S(2)}, u32[]{:S(2)}) collective-permute-start(bf16[32,72,128]{2,1,0:T(8,128)(2,1)S(1)} %all_to_all.5.a0), channel_id=1, source_target_pairs={{0,8},{1,153},{8,16},{9,1},{16,24},{17,9},{24,128},{25,17},{128,13... | collective-permute-start | bytes 1769480 | tf_op jit(solution)/shard_map/ppermute | solution.py:181
  35.9 0.3 collective-permute-start.3
  36.3 0.9 %collective-permute-start.1 = (bf16[32,72,128]{2,1,0:T(8,128)(2,1)S(1)}, bf16[32,72,128]{2,1,0:T(8,128)(2,1)}, u32[]{:S(2)}, u32[]{:S(2)}) collective-permute-start(bf16[32,72,128]{2,1,0:T(8,128)(2,1)S(1)} %all_to_all.5.a0), channel_id=1, source_target_pairs={{0,2},{1,7},{8,10},{9,15},{16,18},{17,23},{24,26},{25,31},{128,130... | collective-permute-start | bytes 1769480 | tf_op jit(solution)/shard_map/ppermute | solution.py:181
  37.2 1.9 %collective-permute-start = (bf16[32,72,128]{2,1,0:T(8,128)(2,1)S(1)}, bf16[32,72,128]{2,1,0:T(8,128)(2,1)S(1)}, u32[]{:S(2)}, u32[]{:S(2)}) collective-permute-start(bf16[32,72,128]{2,1,0:T(8,128)(2,1)S(1)} %all_to_all.5.a0), channel_id=1, source_target_pairs={{0,1},{1,0},{8,9},{9,8},{16,17},{17,16},{24,25},{25,24},{128,129},... | collective-permute-start | bytes 1769480 | tf_op jit(solution)/shard_map/ppermute | solution.py:182
  39.0 3.7 %collective-permute-done.5.a3 = bf16[32,72,128]{2,1,0:T(8,128)(2,1)} collective-permute-done((bf16[32,72,128]{2,1,0:T(8,128)(2,1)S(1)}, bf16[32,72,128]{2,1,0:T(8,128)(2,1)}, u32[]{:S(2)}, u32[]{:S(2)}) %collective-permute-start.5) | collective-permute-done | bytes 589856 | tf_op jit(solution)/shard_map/ppermute | solution.py:181
  42.7 5.8 %collective-permute-start.6 = (bf16[32,72,128]{2,1,0:T(8,128)(2,1)}, bf16[32,72,128]{2,1,0:T(8,128)(2,1)S(1)}, u32[]{:S(2)}, u32[]{:S(2)}) collective-permute-start(bf16[32,72,128]{2,1,0:T(8,128)(2,1)} %collective-permute-done.5.a3), channel_id=1, source_target_pairs={{0,1},{1,0},{8,9},{9,8},{16,17},{17,16},{24,25},{25,24},{128,129},... | collective-permute-start | bytes 1769480 | tf_op jit(solution)/shard_map/ppermute | solution.py:182
  48.6 0.0 collective-permute-done.3.a2
  48.6 0.7 %collective-permute-start.4 = (bf16[32,72,128]{2,1,0:T(8,128)(2,1)}, bf16[32,72,128]{2,1,0:T(8,128)(2,1)S(1)}, u32[]{:S(2)}, u32[]{:S(2)}) collective-permute-start(bf16[32,72,128]{2,1,0:T(8,128)(2,1)} %collective-permute-done.3.a2), channel_id=1, source_target_pairs={{0,1},{1,0},{8,9},{9,8},{16,17},{17,16},{24,25},{25,24},{128,129},... | collective-permute-start | bytes 1769480 | tf_op jit(solution)/shard_map/ppermute | solution.py:182
  49.2 0.0 collective-permute-done.1.a1
  49.2 0.2 collective-permute-start.2
  49.5 0.1 add_add_fusion
  49.5 4.7 %shard_map.37.rest_0_ = bf16[2,2,64,8192]{3,2,1,0:T(8,128)(2,1)} custom-call(s32[4]{0:T(128)S(1)} %get-tuple-element.6.s_ref, bf16[32,72,128]{2,1,0:T(8,128)(2,1)S(1)} %all_to_all.5.a0, bf16[32,72,128]{2,1,0:T(8,128)(2,1)} %collective-permute-done.1.a1, bf16[32,72,128]{2,1,0:T(8,128)(2,1)} %collective-permute-done.3.a2, ...), custom_call_target="tpu_custom_call" | custom-call | flops 268435456 | bytes 6291456 | tf_op jit(solution)/shard_map/pallas_call | solution.py:144
  54.2 0.0 collective-permute-done.a0
  54.2 0.0 collective-permute-done.6.a3
  54.3 0.0 collective-permute-done.4.a2
  54.3 0.0 collective-permute-done.2.a1
  54.3 3.8 %shard_map.38 = bf16[2,2,64,8192]{3,2,1,0:T(8,128)(2,1)} custom-call(s32[4]{0:T(128)S(1)} %get-tuple-element.5.s_ref, bf16[32,72,128]{2,1,0:T(8,128)(2,1)S(1)} %collective-permute-done.a0, bf16[32,72,128]{2,1,0:T(8,128)(2,1)S(1)} %collective-permute-done.2.a1, bf16[32,72,128]{2,1,0:T(8,128)(2,1)S(1)} %collective-permute-done.4.a2, ...), custom_call_target="tpu_custom_call", output_to_operand_aliasing={{}: (6, {})} | custom-call | flops 268435456 | bytes 6291456 | tf_op jit(solution)/shard_map/pallas_call | solution.py:144
  (3 shorter events, 0.0 us)
Async XLA Ops:
  0.0 0.8 %copy-start = (bf16[2,2,64,64]{3,2,1,0:T(8,128)(2,1)S(1)}, bf16[2,2,64,64]{3,2,1,0:T(8,128)(2,1)}, u32[]{:S(2)}) copy-start(bf16[2,2,64,64]{3,2,1,0:T(8,128)(2,1)} %param.3) | copy-start | bytes 98308
  33.3 9.5 %collective-permute-start.5 = (bf16[32,72,128]{2,1,0:T(8,128)(2,1)S(1)}, bf16[32,72,128]{2,1,0:T(8,128)(2,1)}, u32[]{:S(2)}, u32[]{:S(2)}) collective-permute-start(bf16[32,72,128]{2,1,0:T(8,128)(2,1)S(1)} %all_to_all.5.a0), channel_id=1, source_target_pairs={{0,8},{1,153},{8,16},{9,1},{16,24},{17,9},{24,128},{25,17},{128,13... | collective-permute-start | bytes 1769480 | tf_op jit(solution)/shard_map/ppermute | solution.py:181
  35.9 12.6 %collective-permute-start.3 = (bf16[32,72,128]{2,1,0:T(8,128)(2,1)S(1)}, bf16[32,72,128]{2,1,0:T(8,128)(2,1)}, u32[]{:S(2)}, u32[]{:S(2)}) collective-permute-start(bf16[32,72,128]{2,1,0:T(8,128)(2,1)S(1)} %all_to_all.5.a0), channel_id=1, source_target_pairs={{0,32},{1,97},{8,40},{9,105},{16,48},{17,113},{24,56},{25,121},{12... | collective-permute-start | bytes 1769480 | tf_op jit(solution)/shard_map/ppermute | solution.py:181
  36.3 13.0 %collective-permute-start.1 = (bf16[32,72,128]{2,1,0:T(8,128)(2,1)S(1)}, bf16[32,72,128]{2,1,0:T(8,128)(2,1)}, u32[]{:S(2)}, u32[]{:S(2)}) collective-permute-start(bf16[32,72,128]{2,1,0:T(8,128)(2,1)S(1)} %all_to_all.5.a0), channel_id=1, source_target_pairs={{0,2},{1,7},{8,10},{9,15},{16,18},{17,23},{24,26},{25,31},{128,130... | collective-permute-start | bytes 1769480 | tf_op jit(solution)/shard_map/ppermute | solution.py:181
  37.2 17.1 %collective-permute-start = (bf16[32,72,128]{2,1,0:T(8,128)(2,1)S(1)}, bf16[32,72,128]{2,1,0:T(8,128)(2,1)S(1)}, u32[]{:S(2)}, u32[]{:S(2)}) collective-permute-start(bf16[32,72,128]{2,1,0:T(8,128)(2,1)S(1)} %all_to_all.5.a0), channel_id=1, source_target_pairs={{0,1},{1,0},{8,9},{9,8},{16,17},{17,16},{24,25},{25,24},{128,129},... | collective-permute-start | bytes 1769480 | tf_op jit(solution)/shard_map/ppermute | solution.py:182
  42.7 11.5 %collective-permute-start.6 = (bf16[32,72,128]{2,1,0:T(8,128)(2,1)}, bf16[32,72,128]{2,1,0:T(8,128)(2,1)S(1)}, u32[]{:S(2)}, u32[]{:S(2)}) collective-permute-start(bf16[32,72,128]{2,1,0:T(8,128)(2,1)} %collective-permute-done.5.a3), channel_id=1, source_target_pairs={{0,1},{1,0},{8,9},{9,8},{16,17},{17,16},{24,25},{25,24},{128,129},... | collective-permute-start | bytes 1769480 | tf_op jit(solution)/shard_map/ppermute | solution.py:182
  48.6 5.7 %collective-permute-start.4 = (bf16[32,72,128]{2,1,0:T(8,128)(2,1)}, bf16[32,72,128]{2,1,0:T(8,128)(2,1)S(1)}, u32[]{:S(2)}, u32[]{:S(2)}) collective-permute-start(bf16[32,72,128]{2,1,0:T(8,128)(2,1)} %collective-permute-done.3.a2), channel_id=1, source_target_pairs={{0,1},{1,0},{8,9},{9,8},{16,17},{17,16},{24,25},{25,24},{128,129},... | collective-permute-start | bytes 1769480 | tf_op jit(solution)/shard_map/ppermute | solution.py:182
  49.2 5.0 %collective-permute-start.2 = (bf16[32,72,128]{2,1,0:T(8,128)(2,1)}, bf16[32,72,128]{2,1,0:T(8,128)(2,1)S(1)}, u32[]{:S(2)}, u32[]{:S(2)}) collective-permute-start(bf16[32,72,128]{2,1,0:T(8,128)(2,1)} %collective-permute-done.1.a1), channel_id=1, source_target_pairs={{0,1},{1,0},{8,9},{9,8},{16,17},{17,16},{24,25},{25,24},{128,129},... | collective-permute-start | bytes 1769480 | tf_op jit(solution)/shard_map/ppermute | solution.py:182

commit v3 on v2

v3 whole, which is shorter than its diff:
```python
import jax
import jax.numpy as jnp
from jax import lax
from jax.experimental import pallas as pl
from jax.experimental.pallas import tpu as pltpu
from jax.sharding import PartitionSpec as P


AXES = ("train", "tp", "dp")
NX, NY, NZ = 4, 4, 8
H = 64
UP = 8
ROWS = H + UP
CHUNK = 2048
CHUNKS = 4
VMEM_LIMIT = 16 * 1024 * 1024


def linear(x, y, z, c):
    return (((z >> 2) * NY + y) * 16 + (z & 3) * NX + x) * 2 + c


def coords():
    for x in range(NX):
        for y in range(NY):
            for z in range(NZ):
                for c in range(2):
                    yield x, y, z, c


def place(x, y, z, base):
    dz = z ^ base
    far = (dz >> 2) & 1
    near = ((dz >> 1) & 1) ^ far
    member = ((x >> 1) & 1) * 4 + ((y >> 1) & 1) * 2 + (z & 1)
    return member * 4 + near * 2 + far


def colour_groups():
    groups = {}
    for x, y, z, c in coords():
        key = ((x ^ z) & 1, (y ^ z) & 1, z >> 1, c)
        member = ((x >> 1) & 1) * 4 + ((y >> 1) & 1) * 2 + (z & 1)
        groups.setdefault(key, [0] * 8)[member] = linear(x, y, z, c)
    return list(groups.values())


def along_z(flip):
    return [(linear(x, y, z, c), linear(x, y, z ^ flip, c)) for x, y, z, c in coords()]


def from_neighbour(axis):
    pairs = []
    for x, y, z, c in coords():
        q = [x, y, z]
        q[axis] += 1 if c == 0 else -1
        pairs.append((linear(x, y, z, c), linear(q[0] % NX, q[1] % NY, q[2] % NZ, c)))
    return pairs


def other_core():
    return [(linear(x, y, z, c), linear(x, y, z, 1 - c)) for x, y, z, c in coords()]


def merge_layer(layer, mx, my, mz, lists, u_ref, before, w_ref, buf, after):
    px = (mx ^ mz) & 1
    py = (my ^ mz) & 1
    base = (mz, mz, mz, (mz - 1 + 2 * layer) & 7)

    b = (mz & 3) * NX + mx
    y = (b >> 1) & 3
    rows = []
    for j in range(8):
        x = j & 3
        z = (b >> 3) * 4 + (b & 1) * 2 + (j >> 2)
        rel = ((x ^ z ^ px) & 1) + 2 * ((y ^ z ^ py) & 1)
        row = lists[0][place(x, y, z, base[0]), H:ROWS]
        for i in range(1, 4):
            row = jnp.where(rel == i, lists[i][place(x, y, z, base[i]), H:ROWS], row)
        rows.append(row.astype(jnp.float32) * 2.0)
    u = jnp.concatenate(rows, axis=0)
    u = jnp.concatenate([u, u], axis=0)
    r = lax.broadcasted_iota(jnp.int32, u.shape, 0) // 64
    c = lax.broadcasted_iota(jnp.int32, u.shape, 1) // 64
    u_ref[...] = jnp.where(r == c, u, 0.0).astype(jnp.bfloat16)

    for i in range(CHUNKS):
        u = u_ref[...]
        zh, y1 = i >> 1, i & 1
        before(i)
        for y0 in range(2):
            y = y1 * 2 + y0
            for z1 in range(2):
                for kind in range(2):
                    z0 = py ^ (y0 ^ kind)
                    z = zh * 4 + z1 * 2 + z0
                    first = px ^ z0
                    la, lb = lists[2 * kind], lists[2 * kind + 1]
                    parts = []
                    for xh in range(2):
                        even = la[place(2 * xh, y, z, base[2 * kind]), :H]
                        odd = lb[place(2 * xh, y, z, base[2 * kind + 1]), :H]
                        parts.append(jnp.where(first == 0, even, odd))
                        parts.append(jnp.where(first == 0, odd, even))
                    delta = lax.dot_general(
                        u,
                        jnp.concatenate(parts, axis=0),
                        (((1,), (1,)), ((), ())),
                        preferred_element_type=jnp.float32,
                    )
                    at = pl.ds(pl.multiple_of((y0 * 4 + z1 * 2 + z0) * 256, 256), 256)
                    for p in range(2):
                        w = w_ref[i, p, :, at].astype(jnp.float32)
                        buf[i, p, :, at] = (w + delta[p * 64 : p * 64 + 64]).astype(jnp.bfloat16)
        after(i)


def part(ref, layer, i):
    return ref.at[layer, :, :, pl.ds(i * CHUNK, CHUNK)]


def first_kernel(s_ref, a0, a1, a2, a3, w_ref, o_ref, next_ref, held, buf, u_ref, list_sem, load_sem, next_sem, store_sem):
    layer, mx, my, mz = s_ref[0], s_ref[1], s_ref[2], s_ref[3]
    gets = [
        pltpu.make_async_copy(a, held.at[i], list_sem.at[i]) for i, a in enumerate((a0, a1, a2, a3))
    ]
    for get in gets:
        get.start()

    def load(i):
        return pltpu.make_async_copy(part(w_ref, layer, i), buf.at[i], load_sem.at[i])

    def ahead(i):
        return pltpu.make_async_copy(part(w_ref, 1 - layer, i), next_ref.at[i], next_sem.at[i])

    def store(i):
        return pltpu.make_async_copy(buf.at[i], part(o_ref, layer, i), store_sem.at[i])

    for i in range(CHUNKS):
        load(i).start()
    for i in range(CHUNKS):
        ahead(i).start()
    for get in gets:
        get.wait()
    lists = [held.at[i] for i in range(4)]
    merge_layer(
        layer, mx, my, mz, lists, u_ref,
        lambda i: load(i).wait(), buf, buf, lambda i: store(i).start(),
    )
    for i in range(CHUNKS):
        ahead(i).wait()
        store(i).wait()


def second_kernel(s_ref, a0, a1, a2, a3, w_ref, out_ref, o_ref, buf, u_ref, store_sem):
    layer, mx, my, mz = s_ref[0], s_ref[1], s_ref[2], s_ref[3]

    def store(i):
        return pltpu.make_async_copy(buf.at[i], part(o_ref, layer, i), store_sem.at[i])

    merge_layer(
        layer, mx, my, mz, (a0, a1, a2, a3), u_ref,
        lambda i: None, w_ref, buf, lambda i: store(i).start(),
    )
    for i in range(CHUNKS):
        store(i).wait()


SCALARS = pl.BlockSpec(memory_space=pltpu.SMEM)
INSIDE = pl.BlockSpec(memory_space=pltpu.VMEM)
OUTSIDE = pl.BlockSpec(memory_space=pl.ANY)
PARTS = (CHUNKS, 2, 64, CHUNK)
PARAMS = pltpu.CompilerParams(vmem_limit_bytes=VMEM_LIMIT)
COST = pl.CostEstimate(
    flops=2 * 128 * 128 * 8192, bytes_accessed=6 * 1024 * 1024, transcendentals=0
)


def first(scalars, lists, weight):
    return pl.pallas_call(
        first_kernel,
        in_specs=[SCALARS] + [OUTSIDE] * 5,
        out_specs=[OUTSIDE, INSIDE],
        out_shape=[
            jax.ShapeDtypeStruct(weight.shape, weight.dtype),
            jax.ShapeDtypeStruct(PARTS, weight.dtype),
        ],
        scratch_shapes=[
            pltpu.VMEM((4, 32, ROWS, 128), jnp.bfloat16),
            pltpu.VMEM(PARTS, jnp.bfloat16),
            pltpu.VMEM((128, 128), jnp.bfloat16),
            pltpu.SemaphoreType.DMA((4,)),
            pltpu.SemaphoreType.DMA((CHUNKS,)),
            pltpu.SemaphoreType.DMA((CHUNKS,)),
            pltpu.SemaphoreType.DMA((CHUNKS,)),
        ],
        compiler_params=PARAMS,
        cost_estimate=COST,
    )(scalars, *lists, pltpu.with_memory_space_constraint(weight, pltpu.HBM))


def second(scalars, lists, near, out):
    return pl.pallas_call(
        second_kernel,
        in_specs=[SCALARS] + [INSIDE] * 5 + [OUTSIDE],
        out_specs=OUTSIDE,
        out_shape=jax.ShapeDtypeStruct(out.shape, out.dtype),
        scratch_shapes=[
            pltpu.VMEM(PARTS, jnp.bfloat16),
            pltpu.VMEM((128, 128), jnp.bfloat16),
            pltpu.SemaphoreType.DMA((CHUNKS,)),
        ],
        input_output_aliases={6: 0},
        compiler_params=PARAMS,
        cost_estimate=COST,
    )(scalars, *lists, near, out)


def solution(mesh):
    groups = colour_groups()

    def local(down, up, weight):
        core = lax.axis_index("dp")
        train = lax.axis_index("train")
        tp = lax.axis_index("tp")
        x = tp % NX
        y = train % NY
        z = (train // NY) * 4 + tp // NX

        d = lax.dynamic_index_in_dim(down, core, 0, keepdims=False).reshape(128, H).T
        u = lax.dynamic_index_in_dim(up, core, 0, keepdims=False)
        u = u.transpose(1, 0, 2).reshape(UP, 128)
        mine = jnp.concatenate([d, u], axis=0)

        column = mine[None]
        for flip in (6, 2):
            column = jnp.concatenate([column, lax.ppermute(column, AXES, along_z(flip))], axis=0)
        many = jnp.broadcast_to(column[None], (8, 4, ROWS, 128))
        own = lax.all_to_all(many, AXES, 0, 0, axis_index_groups=groups, tiled=True)
        own = own.reshape(32, ROWS, 128)
        lists = [own] + [lax.ppermute(own, AXES, from_neighbour(a)) for a in range(3)]
        swapped = [lax.ppermute(a, AXES, other_core()) for a in lists]

        here = jnp.stack([core, x, y, z]).astype(jnp.int32)
        there = jnp.stack([1 - core, x, y, z]).astype(jnp.int32)
        out, near = first(here, lists, weight)
        return second(there, swapped, near, out)

    spec = P(None, None, "tp", None)
    return jax.shard_map(
        local,
        mesh=mesh,
        in_specs=(
            P(None, None, None, ("train", "tp")),
            P(None, None, ("train", "tp"), None),
            spec,
        ),
        out_specs=spec,
        check_vma=False,
    )
```

time: 58.3 us -> 54 us (0.926)
  blocking collectives: 32.2 us -> 16.7 us
  starting transfers between devices: 12.5 us -> 20.6 us
  waiting for transfers between devices: 3.72 us -> 7.36 us
  Pallas kernels: 8.54 us -> 7.8 us
    all_to_all x1, blocking collectives: 32.2 us -> 16.7 us  [local(): own = lax.all_to_all(many, AXES, 0, 0, axis_index_groups=groups, tiled=True)]
    ppermute x0 -> x2, starting transfers between devices: none -> 8.11 us  [local(): lax.ppermute(column, AXES, along_z(flip))]
    ppermute x0 -> x2, waiting for transfers between devices: none -> 3.69 us  [local(): lax.ppermute(column, AXES, along_z(flip))]
    pallas_call x2, Pallas kernels: 8.54 us -> 7.8 us  [the longest x1 5.45 us: first(): pl.pallas_call(first_kernel, in_specs=[SCALARS] + [OUTSIDE] * 5, out_spec...]
    ppermute x4, starting transfers between devices: 8.57 us -> 7.97 us  [local(): swapped = [lax.ppermute(a, AXES, other_core()) for a in lists]]
  transfers between devices with their start and end apart: 7 -> 9, of which waited for: 1 -> 3; matrix products, arithmetic and copies ran while one was open for 0% -> 0% of each run, Pallas kernels for 8% -> 10%
where the time goes in v3:
time: 54 us; the launch traced here: 53.7 us
  starting transfers between devices  20.6 us (38%)
  blocking collectives  16.7 us (31%)
  Pallas kernels  7.8 us (14%)
  waiting for transfers between devices  7.36 us (14%)
  local copies, waits for them, and re-layouts  1 us (2%)
    all_to_all x1, blocking collectives, local(): own = lax.all_to_all(many, AXES, 0, 0, axis_index_groups=groups, tiled=True)  16.7 us
    ppermute x2, starting transfers between devices, local(): lax.ppermute(column, AXES, along_z(flip))  8.11 us
    ppermute x4, starting transfers between devices, local(): swapped = [lax.ppermute(a, AXES, other_core()) for a in lists]  7.97 us
    pallas_call x1, Pallas kernels, first(): pl.pallas_call(first_kernel, in_specs=[SCALARS] + [OUTSIDE] * 5, out_spec...  5.45 us
    ppermute x3, starting transfers between devices, local(): lax.ppermute(own, AXES, from_neighbour(a))  4.49 us
    ppermute x2, waiting for transfers between devices, local(): lax.ppermute(column, AXES, along_z(flip))  3.69 us
    ppermute x3, waiting for transfers between devices, local(): lax.ppermute(own, AXES, from_neighbour(a))  3.67 us
    pallas_call x1, Pallas kernels, second(): pl.pallas_call(second_kernel, in_specs=[SCALARS] + [INSIDE] * 5 + [OUTSID...  2.35 us
  transfers between devices with their start and end apart: 9, of which 3 were waited for; matrix products, arithmetic and copies ran while one was open for 0% of the time, Pallas kernels for 10%

profile of v3, /device:TPU:1, one launch (start us, length us, event | category | flops | bytes accessed | tf_op | source)
XLA Modules:
  0.0 53.7 jit_solution(7812413256063046909)
XLA Ops:
  0.0 0.0 copy-start
  0.0 0.7 %dynamic-slice_bitcast_fusion = bf16[8,2,64]{2,0,1:T(8,128)(2,1)S(1)} fusion(bf16[2,2,8,64]{3,2,1,0:T(8,128)(2,1)} %param.4, s32[]{:T(128)S(6)} %select_n.28), kind=kLoop, calls=%fused_computation.3 | loop fusion | bytes 4100 | tf_op jit(solution)/shard_map/transpose | solution.py:232
  0.7 0.1 reshape.12
  0.8 0.0 copy-done
  0.8 0.1 copy.8
  1.0 6.9 %collective-permute-start = (bf16[1,72,128]{2,1,0:T(8,128)(2,1)S(1)}, bf16[1,72,128]{2,1,0:T(8,128)(2,1)S(1)}, u32[]{:S(2)}, u32[]{:S(2)}) collective-permute-start(bf16[1,72,128]{2,1,0:T(8,128)(2,1)S(1)} %maximum_bitcast_fusion), channel_id=1, source_target_pairs={{0,144},{1,145},{8,152},{9,153},{16,128},{17,129},{24,136},{25,137... | collective-permute-start | bytes 55304 | tf_op jit(solution)/shard_map/ppermute | solution.py:237
  7.9 1.2 %collective-permute-done = bf16[1,72,128]{2,1,0:T(8,128)(2,1)S(1)} collective-permute-done((bf16[1,72,128]{2,1,0:T(8,128)(2,1)S(1)}, bf16[1,72,128]{2,1,0:T(8,128)(2,1)S(1)}, u32[]{:S(2)}, u32[]{:S(2)}) %collective-permute-start) | collective-permute-done | bytes 18464 | tf_op jit(solution)/shard_map/ppermute | solution.py:237
  9.0 1.2 %collective-permute-start.1 = (bf16[2,72,128]{2,1,0:T(8,128)(2,1)S(1)}, bf16[2,72,128]{2,1,0:T(8,128)(2,1)S(1)}, u32[]{:S(2)}, u32[]{:S(2)}) collective-permute-start(bf16[2,72,128]{2,1,0:T(8,128)(2,1)S(1)} %pad_maximum_fusion.1), channel_id=1, source_target_pairs={{0,16},{1,17},{8,24},{9,25},{16,0},{17,1},{24,8},{25,9},{128,144},... | collective-permute-start | bytes 110600 | tf_op jit(solution)/shard_map/ppermute | solution.py:237
  10.2 2.5 %collective-permute-done.1 = bf16[2,72,128]{2,1,0:T(8,128)(2,1)S(1)} collective-permute-done((bf16[2,72,128]{2,1,0:T(8,128)(2,1)S(1)}, bf16[2,72,128]{2,1,0:T(8,128)(2,1)S(1)}, u32[]{:S(2)}, u32[]{:S(2)}) %collective-permute-start.1) | collective-permute-done | bytes 36896 | tf_op jit(solution)/shard_map/ppermute | solution.py:237
  12.8 0.1 broadcast_in_dim.10
  12.9 16.7 %all_to_all.5 = bf16[8,4,72,128]{3,2,1,0:T(8,128)(2,1)S(1)} all-to-all(bf16[8,4,72,128]{3,2,1,0:T(8,128)(2,1)S(1)} %broadcast_in_dim.10), channel_id=1, replica_groups={{0,42,64,106,4,46,68,110},{1,43,65,107,5,47,69,111},{34,8,98,72,38,12,1..., dimensions={0} | all-to-all | bytes 1179648 | tf_op jit(solution)/shard_map/all_to_all | solution.py:239
  29.6 2.7 %collective-permute-start.7 = (bf16[32,72,128]{2,1,0:T(8,128)(2,1)S(1)}, bf16[32,72,128]{2,1,0:T(8,128)(2,1)}, u32[]{:S(2)}, u32[]{:S(2)}) collective-permute-start(bf16[32,72,128]{2,1,0:T(8,128)(2,1)S(1)} %bitcast.14), channel_id=1, source_target_pairs={{0,8},{1,153},{8,16},{9,1},{16,24},{17,9},{24,128},{25,17},{128,13... | collective-permute-start | bytes 1769480 | tf_op jit(solution)/shard_map/ppermute | solution.py:241
  32.3 0.5 collective-permute-start.5
  32.8 1.3 %collective-permute-start.3 = (bf16[32,72,128]{2,1,0:T(8,128)(2,1)S(1)}, bf16[32,72,128]{2,1,0:T(8,128)(2,1)}, u32[]{:S(2)}, u32[]{:S(2)}) collective-permute-start(bf16[32,72,128]{2,1,0:T(8,128)(2,1)S(1)} %bitcast.16), channel_id=1, source_target_pairs={{0,2},{1,7},{8,10},{9,15},{16,18},{17,23},{24,26},{25,31},{128,130... | collective-permute-start | bytes 1769480 | tf_op jit(solution)/shard_map/ppermute | solution.py:241
  34.1 1.4 %collective-permute-start.2 = (bf16[32,72,128]{2,1,0:T(8,128)(2,1)S(1)}, bf16[32,72,128]{2,1,0:T(8,128)(2,1)S(1)}, u32[]{:S(2)}, u32[]{:S(2)}) collective-permute-start(bf16[32,72,128]{2,1,0:T(8,128)(2,1)S(1)} %bitcast.17), channel_id=1, source_target_pairs={{0,1},{1,0},{8,9},{9,8},{16,17},{17,16},{24,25},{25,24},{128,129},... | collective-permute-start | bytes 1769480 | tf_op jit(solution)/shard_map/ppermute | solution.py:242
  35.5 3.7 %collective-permute-done.7.a3 = bf16[32,72,128]{2,1,0:T(8,128)(2,1)} collective-permute-done((bf16[32,72,128]{2,1,0:T(8,128)(2,1)S(1)}, bf16[32,72,128]{2,1,0:T(8,128)(2,1)}, u32[]{:S(2)}, u32[]{:S(2)}) %collective-permute-start.7) | collective-permute-done | bytes 589856 | tf_op jit(solution)/shard_map/ppermute | solution.py:241
  39.1 5.5 %collective-permute-start.8 = (bf16[32,72,128]{2,1,0:T(8,128)(2,1)}, bf16[32,72,128]{2,1,0:T(8,128)(2,1)S(1)}, u32[]{:S(2)}, u32[]{:S(2)}) collective-permute-start(bf16[32,72,128]{2,1,0:T(8,128)(2,1)} %collective-permute-done.7.a3), channel_id=1, source_target_pairs={{0,1},{1,0},{8,9},{9,8},{16,17},{17,16},{24,25},{25,24},{128,129},... | collective-permute-start | bytes 1769480 | tf_op jit(solution)/shard_map/ppermute | solution.py:242
  44.6 0.0 collective-permute-done.5.a2
  44.6 0.5 collective-permute-start.6
  45.2 0.0 collective-permute-done.3.a1
  45.2 0.6 %collective-permute-start.4 = (bf16[32,72,128]{2,1,0:T(8,128)(2,1)}, bf16[32,72,128]{2,1,0:T(8,128)(2,1)S(1)}, u32[]{:S(2)}, u32[]{:S(2)}) collective-permute-start(bf16[32,72,128]{2,1,0:T(8,128)(2,1)} %collective-permute-done.3.a1), channel_id=1, source_target_pairs={{0,1},{1,0},{8,9},{9,8},{16,17},{17,16},{24,25},{25,24},{128,129},... | collective-permute-start | bytes 1769480 | tf_op jit(solution)/shard_map/ppermute | solution.py:242
  45.7 0.1 add_add_fusion.s_ref
  45.8 0.1 add_add_fusion.1.s_ref
  45.9 5.4 %shard_map.37 = (bf16[2,2,64,8192]{3,2,1,0:T(8,128)(2,1)}, bf16[4,2,64,2048]{3,2,1,0:T(8,128)(2,1)S(1)}) custom-call(s32[4]{0:T(128)S(1)} %add_add_fusion.1.s_ref, bf16[32,72,128]{2,1,0:T(8,128)(2,1)S(1)} %bitcast.18, bf16[32,72,128]{2,1,0:T(8,128)(2,1)} %collective-permute-done.3.a1, bf16[32,72,128]{2,1,0:T(8,128)(2,1)} %collective-permute-done.5.a2, ...), custom_call_target="tpu_custom_call" | custom-call | flops 268435456 | bytes 6291456 | tf_op jit(solution)/shard_map/pallas_call | solution.py:180
  51.3 0.0 collective-permute-done.2.a0
  51.3 0.0 collective-permute-done.8.a3
  51.3 0.0 collective-permute-done.6.a2
  51.4 0.0 collective-permute-done.4.a1
  51.4 2.4 %shard_map.38 = bf16[2,2,64,8192]{3,2,1,0:T(8,128)(2,1)} custom-call(s32[4]{0:T(128)S(1)} %add_add_fusion.s_ref, bf16[32,72,128]{2,1,0:T(8,128)(2,1)S(1)} %collective-permute-done.2.a0, bf16[32,72,128]{2,1,0:T(8,128)(2,1)S(1)} %collective-permute-done.4.a1, bf16[32,72,128]{2,1,0:T(8,128)(2,1)S(1)} %collective-permute-done.6.a2, ...), custom_call_target="tpu_custom_call", output_to_operand_aliasing={{}: (6, {})} | custom-call | flops 268435456 | bytes 6291456 | tf_op jit(solution)/shard_map/pallas_call | solution.py:203
  (5 shorter events, 0.0 us)
Async XLA Ops:
  0.0 0.8 %copy-start = (bf16[2,2,64,64]{3,2,1,0:T(8,128)(2,1)S(1)}, bf16[2,2,64,64]{3,2,1,0:T(8,128)(2,1)}, u32[]{:S(2)}) copy-start(bf16[2,2,64,64]{3,2,1,0:T(8,128)(2,1)} %param.3) | copy-start | bytes 98308
  1.0 8.1 %collective-permute-start = (bf16[1,72,128]{2,1,0:T(8,128)(2,1)S(1)}, bf16[1,72,128]{2,1,0:T(8,128)(2,1)S(1)}, u32[]{:S(2)}, u32[]{:S(2)}) collective-permute-start(bf16[1,72,128]{2,1,0:T(8,128)(2,1)S(1)} %maximum_bitcast_fusion), channel_id=1, source_target_pairs={{0,144},{1,145},{8,152},{9,153},{16,128},{17,129},{24,136},{25,137... | collective-permute-start | bytes 55304 | tf_op jit(solution)/shard_map/ppermute | solution.py:237
  9.0 3.7 %collective-permute-start.1 = (bf16[2,72,128]{2,1,0:T(8,128)(2,1)S(1)}, bf16[2,72,128]{2,1,0:T(8,128)(2,1)S(1)}, u32[]{:S(2)}, u32[]{:S(2)}) collective-permute-start(bf16[2,72,128]{2,1,0:T(8,128)(2,1)S(1)} %pad_maximum_fusion.1), channel_id=1, source_target_pairs={{0,16},{1,17},{8,24},{9,25},{16,0},{17,1},{24,8},{25,9},{128,144},... | collective-permute-start | bytes 110600 | tf_op jit(solution)/shard_map/ppermute | solution.py:237
  29.6 9.5 %collective-permute-start.7 = (bf16[32,72,128]{2,1,0:T(8,128)(2,1)S(1)}, bf16[32,72,128]{2,1,0:T(8,128)(2,1)}, u32[]{:S(2)}, u32[]{:S(2)}) collective-permute-start(bf16[32,72,128]{2,1,0:T(8,128)(2,1)S(1)} %bitcast.14), channel_id=1, source_target_pairs={{0,8},{1,153},{8,16},{9,1},{16,24},{17,9},{24,128},{25,17},{128,13... | collective-permute-start | bytes 1769480 | tf_op jit(solution)/shard_map/ppermute | solution.py:241
  32.3 12.3 %collective-permute-start.5 = (bf16[32,72,128]{2,1,0:T(8,128)(2,1)S(1)}, bf16[32,72,128]{2,1,0:T(8,128)(2,1)}, u32[]{:S(2)}, u32[]{:S(2)}) collective-permute-start(bf16[32,72,128]{2,1,0:T(8,128)(2,1)S(1)} %bitcast.15), channel_id=1, source_target_pairs={{0,32},{1,97},{8,40},{9,105},{16,48},{17,113},{24,56},{25,121},{12... | collective-permute-start | bytes 1769480 | tf_op jit(solution)/shard_map/ppermute | solution.py:241
  32.8 12.4 %collective-permute-start.3 = (bf16[32,72,128]{2,1,0:T(8,128)(2,1)S(1)}, bf16[32,72,128]{2,1,0:T(8,128)(2,1)}, u32[]{:S(2)}, u32[]{:S(2)}) collective-permute-start(bf16[32,72,128]{2,1,0:T(8,128)(2,1)S(1)} %bitcast.16), channel_id=1, source_target_pairs={{0,2},{1,7},{8,10},{9,15},{16,18},{17,23},{24,26},{25,31},{128,130... | collective-permute-start | bytes 1769480 | tf_op jit(solution)/shard_map/ppermute | solution.py:241
  34.1 17.3 %collective-permute-start.2 = (bf16[32,72,128]{2,1,0:T(8,128)(2,1)S(1)}, bf16[32,72,128]{2,1,0:T(8,128)(2,1)S(1)}, u32[]{:S(2)}, u32[]{:S(2)}) collective-permute-start(bf16[32,72,128]{2,1,0:T(8,128)(2,1)S(1)} %bitcast.17), channel_id=1, source_target_pairs={{0,1},{1,0},{8,9},{9,8},{16,17},{17,16},{24,25},{25,24},{128,129},... | collective-permute-start | bytes 1769480 | tf_op jit(solution)/shard_map/ppermute | solution.py:242
  39.1 12.2 %collective-permute-start.8 = (bf16[32,72,128]{2,1,0:T(8,128)(2,1)}, bf16[32,72,128]{2,1,0:T(8,128)(2,1)S(1)}, u32[]{:S(2)}, u32[]{:S(2)}) collective-permute-start(bf16[32,72,128]{2,1,0:T(8,128)(2,1)} %collective-permute-done.7.a3), channel_id=1, source_target_pairs={{0,1},{1,0},{8,9},{9,8},{16,17},{17,16},{24,25},{25,24},{128,129},... | collective-permute-start | bytes 1769480 | tf_op jit(solution)/shard_map/ppermute | solution.py:242
  44.6 6.7 %collective-permute-start.6 = (bf16[32,72,128]{2,1,0:T(8,128)(2,1)}, bf16[32,72,128]{2,1,0:T(8,128)(2,1)S(1)}, u32[]{:S(2)}, u32[]{:S(2)}) collective-permute-start(bf16[32,72,128]{2,1,0:T(8,128)(2,1)} %collective-permute-done.5.a2), channel_id=1, source_target_pairs={{0,1},{1,0},{8,9},{9,8},{16,17},{17,16},{24,25},{25,24},{128,129},... | collective-permute-start | bytes 1769480 | tf_op jit(solution)/shard_map/ppermute | solution.py:242
  45.2 6.2 %collective-permute-start.4 = (bf16[32,72,128]{2,1,0:T(8,128)(2,1)}, bf16[32,72,128]{2,1,0:T(8,128)(2,1)S(1)}, u32[]{:S(2)}, u32[]{:S(2)}) collective-permute-start(bf16[32,72,128]{2,1,0:T(8,128)(2,1)} %collective-permute-done.3.a1), channel_id=1, source_target_pairs={{0,1},{1,0},{8,9},{9,8},{16,17},{17,16},{24,25},{25,24},{128,129},... | collective-permute-start | bytes 1769480 | tf_op jit(solution)/shard_map/ppermute | solution.py:242

commit v4 on v2

v4 whole, which is shorter than its diff:
```python
import jax
import jax.numpy as jnp
from jax import lax
from jax.experimental import pallas as pl
from jax.experimental.pallas import tpu as pltpu
from jax.sharding import PartitionSpec as P


AXES = ("train", "tp", "dp")
NX, NY, NZ = 4, 4, 8
H = 64
UP = 8
ROWS = H + UP
CHUNK = 2048
CHUNKS = 4
VMEM_LIMIT = 16 * 1024 * 1024


def linear(x, y, z, c):
    return (((z >> 2) * NY + y) * 16 + (z & 3) * NX + x) * 2 + c


def coords():
    for x in range(NX):
        for y in range(NY):
            for z in range(NZ):
                for c in range(2):
                    yield x, y, z, c


def place(x, y, z, base):
    dz = z ^ base
    far = (dz >> 2) & 1
    near = ((dz >> 1) & 1) ^ far
    member = ((x >> 1) & 1) * 4 + ((y >> 1) & 1) * 2 + (z & 1)
    return member * 4 + near * 2 + far


def colour_groups():
    groups = {}
    for x, y, z, c in coords():
        key = ((x ^ z) & 1, (y ^ z) & 1, z >> 1, c)
        member = ((x >> 1) & 1) * 4 + ((y >> 1) & 1) * 2 + (z & 1)
        groups.setdefault(key, [0] * 8)[member] = linear(x, y, z, c)
    return list(groups.values())


def along_z(flip):
    return [(linear(x, y, z, c), linear(x, y, z ^ flip, c)) for x, y, z, c in coords()]


def from_neighbour(axis):
    pairs = []
    for x, y, z, c in coords():
        q = [x, y, z]
        q[axis] += 1 if c == 0 else -1
        pairs.append((linear(x, y, z, c), linear(q[0] % NX, q[1] % NY, q[2] % NZ, c)))
    return pairs


def other_core():
    return [(linear(x, y, z, c), linear(x, y, z, 1 - c)) for x, y, z, c in coords()]


def fetch_kernel(own_ref, w_ref, o_ref, token_ref, sem):
    copies = [
        pltpu.make_async_copy(part(w_ref, layer, i), o_ref.at[layer, i], sem.at[layer * CHUNKS + i])
        for layer in range(2)
        for i in range(CHUNKS)
    ]
    for copy in copies:
        copy.start()
    token_ref[...] = jnp.zeros_like(token_ref)
    for copy in copies:
        copy.wait()


def part(ref, layer, i):
    return ref.at[layer, :, :, pl.ds(i * CHUNK, CHUNK)]


def fetch(own, weight):
    inside = pl.BlockSpec(memory_space=pltpu.VMEM)
    outside = pl.BlockSpec(memory_space=pl.ANY)
    return pl.pallas_call(
        fetch_kernel,
        in_specs=[outside] * 2,
        out_specs=[inside] * 2,
        out_shape=[
            jax.ShapeDtypeStruct((2, CHUNKS, 2, 64, CHUNK), weight.dtype),
            jax.ShapeDtypeStruct((8, 128), jnp.float32),
        ],
        scratch_shapes=[pltpu.SemaphoreType.DMA((2 * CHUNKS,))],
        compiler_params=pltpu.CompilerParams(vmem_limit_bytes=VMEM_LIMIT),
        cost_estimate=pl.CostEstimate(flops=0, bytes_accessed=8 * 1024 * 1024, transcendentals=0),
    )(own, pltpu.with_memory_space_constraint(weight, pltpu.HBM))


def merge_kernel(s_ref, a0, a1, a2, a3, w_ref, *rest):
    lists = (a0, a1, a2, a3)
    o_ref, buf, u_ref, sem = rest[-4:]
    layer, mx, my, mz = s_ref[0], s_ref[1], s_ref[2], s_ref[3]
    px = (mx ^ mz) & 1
    py = (my ^ mz) & 1
    base = (mz, mz, mz, (mz - 1 + 2 * layer) & 7)

    def take(i, x, y, z, rows):
        return lists[i][place(x, y, z, base[i]), rows]

    b = (mz & 3) * NX + mx
    y = (b >> 1) & 3
    rows = []
    for j in range(8):
        x = j & 3
        z = (b >> 3) * 4 + (b & 1) * 2 + (j >> 2)
        rel = ((x ^ z ^ px) & 1) + 2 * ((y ^ z ^ py) & 1)
        row = take(0, x, y, z, slice(H, ROWS))
        for i in range(1, 4):
            row = jnp.where(rel == i, take(i, x, y, z, slice(H, ROWS)), row)
        rows.append(row.astype(jnp.float32) * 2.0)
    u = jnp.concatenate(rows, axis=0)
    u = jnp.concatenate([u, u], axis=0)
    r = lax.broadcasted_iota(jnp.int32, u.shape, 0) // 64
    c = lax.broadcasted_iota(jnp.int32, u.shape, 1) // 64
    u_ref[...] = jnp.where(r == c, u, 0.0).astype(jnp.bfloat16)

    def store(i):
        return pltpu.make_async_copy(buf.at[i], part(o_ref, layer, i), sem.at[i])

    for i in range(CHUNKS):
        u = u_ref[...]
        zh, y1 = i >> 1, i & 1
        for y0 in range(2):
            y = y1 * 2 + y0
            for z1 in range(2):
                for kind in range(2):
                    z0 = py ^ (y0 ^ kind)
                    z = zh * 4 + z1 * 2 + z0
                    first = px ^ z0
                    parts = []
                    for xh in range(2):
                        even = take(2 * kind, 2 * xh, y, z, slice(0, H))
                        odd = take(2 * kind + 1, 2 * xh, y, z, slice(0, H))
                        parts.append(jnp.where(first == 0, even, odd))
                        parts.append(jnp.where(first == 0, odd, even))
                    delta = lax.dot_general(
                        u,
                        jnp.concatenate(parts, axis=0),
                        (((1,), (1,)), ((), ())),
                        preferred_element_type=jnp.float32,
                    )
                    at = pl.ds(pl.multiple_of((y0 * 4 + z1 * 2 + z0) * 256, 256), 256)
                    for p in range(2):
                        w = w_ref[layer, i, p, :, at].astype(jnp.float32)
                        buf[i, p, :, at] = (w + delta[p * 64 : p * 64 + 64]).astype(jnp.bfloat16)
        store(i).start()
    for i in range(CHUNKS):
        store(i).wait()


def merge(scalars, lists, near, shape, out=None):
    inside = pl.BlockSpec(memory_space=pltpu.VMEM)
    outside = pl.BlockSpec(memory_space=pl.ANY)
    args = [scalars, *lists, near]
    in_specs = [pl.BlockSpec(memory_space=pltpu.SMEM)] + [inside] * (len(args) - 1)
    aliases = {}
    if out is not None:
        aliases = {len(args): 0}
        in_specs.append(outside)
        args.append(out)
    return pl.pallas_call(
        merge_kernel,
        in_specs=in_specs,
        out_specs=outside,
        out_shape=jax.ShapeDtypeStruct(shape, jnp.bfloat16),
        scratch_shapes=[
            pltpu.VMEM((CHUNKS, 2, 64, CHUNK), jnp.bfloat16),
            pltpu.VMEM((128, 128), jnp.bfloat16),
            pltpu.SemaphoreType.DMA((CHUNKS,)),
        ],
        input_output_aliases=aliases,
        compiler_params=pltpu.CompilerParams(vmem_limit_bytes=VMEM_LIMIT),
        cost_estimate=pl.CostEstimate(
            flops=2 * 128 * 128 * 8192, bytes_accessed=6 * 1024 * 1024, transcendentals=0
        ),
    )(*args)


def solution(mesh):
    groups = colour_groups()

    def local(down, up, weight):
        core = lax.axis_index("dp")
        train = lax.axis_index("train")
        tp = lax.axis_index("tp")
        x = tp % NX
        y = train % NY
        z = (train // NY) * 4 + tp // NX

        d = lax.dynamic_index_in_dim(down, core, 0, keepdims=False).reshape(128, H).T
        u = lax.dynamic_index_in_dim(up, core, 0, keepdims=False)
        u = u.transpose(1, 0, 2).reshape(UP, 128)
        mine = jnp.concatenate([d, u], axis=0)

        here = jnp.stack([core, x, y, z]).astype(jnp.int32)
        there = jnp.stack([1 - core, x, y, z]).astype(jnp.int32)
        mine, here, there = lax.optimization_barrier((mine, here, there))

        column = mine[None]
        for flip in (6, 2):
            column = jnp.concatenate([column, lax.ppermute(column, AXES, along_z(flip))], axis=0)
        many = jnp.broadcast_to(column[None], (8, 4, ROWS, 128))
        own = lax.all_to_all(many, AXES, 0, 0, axis_index_groups=groups, tiled=True)
        own = own.reshape(32, ROWS, 128)
        near, token = fetch(own, weight)
        lists = [lax.ppermute(own, AXES, from_neighbour(a)) for a in range(3)]
        lists = [own] + [lax.optimization_barrier((token, a))[1] for a in lists]
        swapped = [lax.ppermute(a, AXES, other_core()) for a in lists]

        out = merge(here, lists, near, weight.shape)
        return merge(there, swapped, near, weight.shape, out)

    spec = P(None, None, "tp", None)
    return jax.shard_map(
        local,
        mesh=mesh,
        in_specs=(
            P(None, None, None, ("train", "tp")),
            P(None, None, ("train", "tp"), None),
            spec,
        ),
        out_specs=spec,
        check_vma=False,
    )
```

time: 58.3 us -> 51.6 us (0.89)
  blocking collectives: 32.2 us -> 16.7 us
  starting transfers between devices: 12.5 us -> 18.2 us
  waiting for transfers between devices: 3.72 us -> 7.66 us
  Pallas kernels: 8.54 us -> 7.51 us
    all_to_all x1, blocking collectives: 32.2 us -> 16.7 us  [local(): own = lax.all_to_all(many, AXES, 0, 0, axis_index_groups=groups, tiled=True)]
    ppermute x3 -> x5, starting transfers between devices: 3.91 us -> 12.5 us  [the longest x2 8.05 us: local(): lax.ppermute(column, AXES, along_z(flip))]
    pallas_call x2, Pallas kernels: 8.54 us -> 4.7 us  [merge(): pl.pallas_call(merge_kernel, in_specs=in_specs, out_specs=outside, out_sh...]
    ppermute x3 -> x5, waiting for transfers between devices: 3.71 us -> 7.24 us  [the longest x2 3.69 us: local(): lax.ppermute(column, AXES, along_z(flip))]
    ppermute x4, starting transfers between devices: 8.57 us -> 5.67 us  [local(): swapped = [lax.ppermute(a, AXES, other_core()) for a in lists]]
    pallas_call x0 -> x1, Pallas kernels: none -> 2.81 us  [fetch(): pl.pallas_call(fetch_kernel, in_specs=[outside] * 2, out_specs=[inside] *...]
  transfers between devices with their start and end apart: 7 -> 9, of which waited for: 1 -> 6; matrix products, arithmetic and copies ran while one was open for 0% -> 0% of each run, Pallas kernels for 8% -> 10%
where the time goes in v4:
time: 51.6 us; the launch traced here: 51.3 us
  starting transfers between devices  18.2 us (35%)
  blocking collectives  16.7 us (32%)
  waiting for transfers between devices  7.66 us (15%)
  Pallas kernels  7.51 us (15%)
  local copies, waits for them, and re-layouts  1 us (2%)
    all_to_all x1, blocking collectives, local(): own = lax.all_to_all(many, AXES, 0, 0, axis_index_groups=groups, tiled=True)  16.7 us
    ppermute x2, starting transfers between devices, local(): lax.ppermute(column, AXES, along_z(flip))  8.05 us
    ppermute x4, starting transfers between devices, local(): swapped = [lax.ppermute(a, AXES, other_core()) for a in lists]  5.67 us
    pallas_call x2, Pallas kernels, merge(): pl.pallas_call(merge_kernel, in_specs=in_specs, out_specs=outside, out_sh...  4.7 us
    ppermute x3, starting transfers between devices, local(): lists = [lax.ppermute(own, AXES, from_neighbour(a)) for a in range(3)]  4.49 us
    ppermute x2, waiting for transfers between devices, local(): lax.ppermute(column, AXES, along_z(flip))  3.69 us
    ppermute x3, waiting for transfers between devices, local(): lists = [lax.ppermute(own, AXES, from_neighbour(a)) for a in range(3)]  3.56 us
    pallas_call x1, Pallas kernels, fetch(): pl.pallas_call(fetch_kernel, in_specs=[outside] * 2, out_specs=[inside] *...  2.81 us
  transfers between devices with their start and end apart: 9, of which 6 were waited for; matrix products, arithmetic and copies ran while one was open for 0% of the time, Pallas kernels for 10%

profile of v4, /device:TPU:1, one launch (start us, length us, event | category | flops | bytes accessed | tf_op | source)
XLA Modules:
  0.0 51.3 jit_solution(15408258954458555698)
XLA Ops:
  0.0 0.0 copy-start
  0.0 0.7 %dynamic-slice_bitcast_fusion = bf16[8,2,64]{2,0,1:T(8,128)(2,1)S(1)} fusion(bf16[2,2,8,64]{3,2,1,0:T(8,128)(2,1)} %param.4, s32[]{:T(128)S(6)} %select_n.24), kind=kLoop, calls=%fused_computation.3 | loop fusion | bytes 4100 | tf_op jit(solution)/shard_map/transpose | solution.py:202
  0.7 0.1 reshape.12
  0.8 0.0 copy-done
  0.8 0.1 copy.8
  1.0 0.1 add_add_fusion
  1.1 6.9 %collective-permute-start = (bf16[1,72,128]{2,1,0:T(8,128)(2,1)S(1)}, bf16[1,72,128]{2,1,0:T(8,128)(2,1)S(1)}, u32[]{:S(2)}, u32[]{:S(2)}) collective-permute-start(bf16[1,72,128]{2,1,0:T(8,128)(2,1)S(1)} %bitcast.19), channel_id=1, source_target_pairs={{0,144},{1,145},{8,152},{9,153},{16,128},{17,129},{24,136},{25,137... | collective-permute-start | bytes 55304 | tf_op jit(solution)/shard_map/ppermute | solution.py:211
  7.9 1.2 %collective-permute-done = bf16[1,72,128]{2,1,0:T(8,128)(2,1)S(1)} collective-permute-done((bf16[1,72,128]{2,1,0:T(8,128)(2,1)S(1)}, bf16[1,72,128]{2,1,0:T(8,128)(2,1)S(1)}, u32[]{:S(2)}, u32[]{:S(2)}) %collective-permute-start) | collective-permute-done | bytes 18464 | tf_op jit(solution)/shard_map/ppermute | solution.py:211
  9.1 1.2 %collective-permute-start.1 = (bf16[2,72,128]{2,1,0:T(8,128)(2,1)S(1)}, bf16[2,72,128]{2,1,0:T(8,128)(2,1)S(1)}, u32[]{:S(2)}, u32[]{:S(2)}) collective-permute-start(bf16[2,72,128]{2,1,0:T(8,128)(2,1)S(1)} %pad_maximum_fusion.1), channel_id=1, source_target_pairs={{0,16},{1,17},{8,24},{9,25},{16,0},{17,1},{24,8},{25,9},{128,144},... | collective-permute-start | bytes 110600 | tf_op jit(solution)/shard_map/ppermute | solution.py:211
  10.3 2.5 %collective-permute-done.1 = bf16[2,72,128]{2,1,0:T(8,128)(2,1)S(1)} collective-permute-done((bf16[2,72,128]{2,1,0:T(8,128)(2,1)S(1)}, bf16[2,72,128]{2,1,0:T(8,128)(2,1)S(1)}, u32[]{:S(2)}, u32[]{:S(2)}) %collective-permute-start.1) | collective-permute-done | bytes 36896 | tf_op jit(solution)/shard_map/ppermute | solution.py:211
  12.8 0.1 broadcast_in_dim.10
  12.9 16.7 %all_to_all.5 = bf16[8,4,72,128]{3,2,1,0:T(8,128)(2,1)S(1)} all-to-all(bf16[8,4,72,128]{3,2,1,0:T(8,128)(2,1)S(1)} %broadcast_in_dim.10), channel_id=1, replica_groups={{0,42,64,106,4,46,68,110},{1,43,65,107,5,47,69,111},{34,8,98,72,38,12,1..., dimensions={0} | all-to-all | bytes 1179648 | tf_op jit(solution)/shard_map/all_to_all | solution.py:213
  29.6 2.7 %collective-permute-start.7 = (bf16[32,72,128]{2,1,0:T(8,128)(2,1)S(1)}, bf16[32,72,128]{2,1,0:T(8,128)(2,1)S(1)}, u32[]{:S(2)}, u32[]{:S(2)}) collective-permute-start(bf16[32,72,128]{2,1,0:T(8,128)(2,1)S(1)} %bitcast.13), channel_id=1, source_target_pairs={{0,8},{1,153},{8,16},{9,1},{16,24},{17,9},{24,128},{25,17},{128,13... | collective-permute-start | bytes 1769480 | tf_op jit(solution)/shard_map/ppermute | solution.py:216
  32.3 0.5 collective-permute-start.5
  32.8 1.3 %collective-permute-start.3 = (bf16[32,72,128]{2,1,0:T(8,128)(2,1)S(1)}, bf16[32,72,128]{2,1,0:T(8,128)(2,1)S(1)}, u32[]{:S(2)}, u32[]{:S(2)}) collective-permute-start(bf16[32,72,128]{2,1,0:T(8,128)(2,1)S(1)} %bitcast.15), channel_id=1, source_target_pairs={{0,2},{1,7},{8,10},{9,15},{16,18},{17,23},{24,26},{25,31},{128,130... | collective-permute-start | bytes 1769480 | tf_op jit(solution)/shard_map/ppermute | solution.py:216
  34.1 1.4 %collective-permute-start.2 = (bf16[32,72,128]{2,1,0:T(8,128)(2,1)S(1)}, bf16[32,72,128]{2,1,0:T(8,128)(2,1)S(1)}, u32[]{:S(2)}, u32[]{:S(2)}) collective-permute-start(bf16[32,72,128]{2,1,0:T(8,128)(2,1)S(1)} %bitcast.16), channel_id=1, source_target_pairs={{0,1},{1,0},{8,9},{9,8},{16,17},{17,16},{24,25},{25,24},{128,129},... | collective-permute-start | bytes 1769480 | tf_op jit(solution)/shard_map/ppermute | solution.py:218
  35.5 2.8 %shard_map.37 = (bf16[2,4,2,64,2048]{4,3,2,1,0:T(8,128)(2,1)S(1)}, f32[8,128]{1,0:T(8,128)}) custom-call(bf16[32,72,128]{2,1,0:T(8,128)(2,1)S(1)} %bitcast.17, bf16[2,2,64,8192]{3,2,1,0:T(8,128)(2,1)} %w_ref.1), custom_call_target="tpu_custom_call" | custom-call | bytes 8388608 | tf_op jit(solution)/shard_map/pallas_call | solution.py:85
  38.3 0.8 %collective-permute-done.7.a3 = bf16[32,72,128]{2,1,0:T(8,128)(2,1)S(1)} collective-permute-done((bf16[32,72,128]{2,1,0:T(8,128)(2,1)S(1)}, bf16[32,72,128]{2,1,0:T(8,128)(2,1)S(1)}, u32[]{:S(2)}, u32[]{:S(2)}) %collective-permute-start.7) | collective-permute-done | bytes 589856 | tf_op jit(solution)/shard_map/ppermute | solution.py:216
  39.2 2.2 %collective-permute-done.5.a2 = bf16[32,72,128]{2,1,0:T(8,128)(2,1)S(1)} collective-permute-done((bf16[32,72,128]{2,1,0:T(8,128)(2,1)S(1)}, bf16[32,72,128]{2,1,0:T(8,128)(2,1)S(1)}, u32[]{:S(2)}, u32[]{:S(2)}) %collective-permute-start.5) | collective-permute-done | bytes 589856 | tf_op jit(solution)/shard_map/ppermute | solution.py:216
  41.4 0.5 %collective-permute-done.3.a1 = bf16[32,72,128]{2,1,0:T(8,128)(2,1)S(1)} collective-permute-done((bf16[32,72,128]{2,1,0:T(8,128)(2,1)S(1)}, bf16[32,72,128]{2,1,0:T(8,128)(2,1)S(1)}, u32[]{:S(2)}, u32[]{:S(2)}) %collective-permute-start.3) | collective-permute-done | bytes 589856 | tf_op jit(solution)/shard_map/ppermute | solution.py:216
  41.9 3.8 %collective-permute-start.4 = (bf16[32,72,128]{2,1,0:T(8,128)(2,1)S(1)}, bf16[32,72,128]{2,1,0:T(8,128)(2,1)S(1)}, u32[]{:S(2)}, u32[]{:S(2)}) collective-permute-start(bf16[32,72,128]{2,1,0:T(8,128)(2,1)S(1)} %collective-permute-done.3.a1), channel_id=1, source_target_pairs={{0,1},{1,0},{8,9},{9,8},{16,17},{17,16},{24,25},{25,24},{128,129},... | collective-permute-start | bytes 1769480 | tf_op jit(solution)/shard_map/ppermute | solution.py:218
  45.6 0.0 collective-permute-start.6
  45.7 0.5 collective-permute-start.8
  46.2 2.4 %shard_map.38.rest_0_ = bf16[2,2,64,8192]{3,2,1,0:T(8,128)(2,1)} custom-call(s32[4]{0:T(128)S(1)} %get-tuple-element.20.s_ref, bf16[32,72,128]{2,1,0:T(8,128)(2,1)S(1)} %bitcast.18, bf16[32,72,128]{2,1,0:T(8,128)(2,1)S(1)} %collective-permute-done.3.a1, bf16[32,72,128]{2,1,0:T(8,128)(2,1)S(1)} %collective-permute-done.5.a2, ...), custom_call_target="tpu_custom_call" | custom-call | flops 268435456 | bytes 6291456 | tf_op jit(solution)/shard_map/pallas_call | solution.py:171
  48.5 0.0 collective-permute-done.2.a0
  48.5 0.0 collective-permute-done.4.a1
  48.5 0.0 collective-permute-done.6.a2
  48.6 0.4 collective-permute-done.8.a3
  49.0 2.3 %shard_map.39 = bf16[2,2,64,8192]{3,2,1,0:T(8,128)(2,1)} custom-call(s32[4]{0:T(128)S(1)} %get-tuple-element.13.s_ref, bf16[32,72,128]{2,1,0:T(8,128)(2,1)S(1)} %collective-permute-done.2.a0, bf16[32,72,128]{2,1,0:T(8,128)(2,1)S(1)} %collective-permute-done.4.a1, bf16[32,72,128]{2,1,0:T(8,128)(2,1)S(1)} %collective-permute-done.6.a2, ...), custom_call_target="tpu_custom_call", output_to_operand_aliasing={{}: (6, {})} | custom-call | flops 268435456 | bytes 6291456 | tf_op jit(solution)/shard_map/pallas_call | solution.py:171
  (5 shorter events, 0.0 us)
Async XLA Ops:
  0.0 0.8 %copy-start = (bf16[2,2,64,64]{3,2,1,0:T(8,128)(2,1)S(1)}, bf16[2,2,64,64]{3,2,1,0:T(8,128)(2,1)}, u32[]{:S(2)}) copy-start(bf16[2,2,64,64]{3,2,1,0:T(8,128)(2,1)} %param.3) | copy-start | bytes 98308
  1.1 8.0 %collective-permute-start = (bf16[1,72,128]{2,1,0:T(8,128)(2,1)S(1)}, bf16[1,72,128]{2,1,0:T(8,128)(2,1)S(1)}, u32[]{:S(2)}, u32[]{:S(2)}) collective-permute-start(bf16[1,72,128]{2,1,0:T(8,128)(2,1)S(1)} %bitcast.19), channel_id=1, source_target_pairs={{0,144},{1,145},{8,152},{9,153},{16,128},{17,129},{24,136},{25,137... | collective-permute-start | bytes 55304 | tf_op jit(solution)/shard_map/ppermute | solution.py:211
  9.1 3.7 %collective-permute-start.1 = (bf16[2,72,128]{2,1,0:T(8,128)(2,1)S(1)}, bf16[2,72,128]{2,1,0:T(8,128)(2,1)S(1)}, u32[]{:S(2)}, u32[]{:S(2)}) collective-permute-start(bf16[2,72,128]{2,1,0:T(8,128)(2,1)S(1)} %pad_maximum_fusion.1), channel_id=1, source_target_pairs={{0,16},{1,17},{8,24},{9,25},{16,0},{17,1},{24,8},{25,9},{128,144},... | collective-permute-start | bytes 110600 | tf_op jit(solution)/shard_map/ppermute | solution.py:211
  29.6 9.5 %collective-permute-start.7 = (bf16[32,72,128]{2,1,0:T(8,128)(2,1)S(1)}, bf16[32,72,128]{2,1,0:T(8,128)(2,1)S(1)}, u32[]{:S(2)}, u32[]{:S(2)}) collective-permute-start(bf16[32,72,128]{2,1,0:T(8,128)(2,1)S(1)} %bitcast.13), channel_id=1, source_target_pairs={{0,8},{1,153},{8,16},{9,1},{16,24},{17,9},{24,128},{25,17},{128,13... | collective-permute-start | bytes 1769480 | tf_op jit(solution)/shard_map/ppermute | solution.py:216
  32.3 9.0 %collective-permute-start.5 = (bf16[32,72,128]{2,1,0:T(8,128)(2,1)S(1)}, bf16[32,72,128]{2,1,0:T(8,128)(2,1)S(1)}, u32[]{:S(2)}, u32[]{:S(2)}) collective-permute-start(bf16[32,72,128]{2,1,0:T(8,128)(2,1)S(1)} %bitcast.14), channel_id=1, source_target_pairs={{0,32},{1,97},{8,40},{9,105},{16,48},{17,113},{24,56},{25,121},{12... | collective-permute-start | bytes 1769480 | tf_op jit(solution)/shard_map/ppermute | solution.py:216
  32.8 9.1 %collective-permute-start.3 = (bf16[32,72,128]{2,1,0:T(8,128)(2,1)S(1)}, bf16[32,72,128]{2,1,0:T(8,128)(2,1)S(1)}, u32[]{:S(2)}, u32[]{:S(2)}) collective-permute-start(bf16[32,72,128]{2,1,0:T(8,128)(2,1)S(1)} %bitcast.15), channel_id=1, source_target_pairs={{0,2},{1,7},{8,10},{9,15},{16,18},{17,23},{24,26},{25,31},{128,130... | collective-permute-start | bytes 1769480 | tf_op jit(solution)/shard_map/ppermute | solution.py:216
  34.1 14.4 %collective-permute-start.2 = (bf16[32,72,128]{2,1,0:T(8,128)(2,1)S(1)}, bf16[32,72,128]{2,1,0:T(8,128)(2,1)S(1)}, u32[]{:S(2)}, u32[]{:S(2)}) collective-permute-start(bf16[32,72,128]{2,1,0:T(8,128)(2,1)S(1)} %bitcast.16), channel_id=1, source_target_pairs={{0,1},{1,0},{8,9},{9,8},{16,17},{17,16},{24,25},{25,24},{128,129},... | collective-permute-start | bytes 1769480 | tf_op jit(solution)/shard_map/ppermute | solution.py:218
  41.9 6.6 %collective-permute-start.4 = (bf16[32,72,128]{2,1,0:T(8,128)(2,1)S(1)}, bf16[32,72,128]{2,1,0:T(8,128)(2,1)S(1)}, u32[]{:S(2)}, u32[]{:S(2)}) collective-permute-start(bf16[32,72,128]{2,1,0:T(8,128)(2,1)S(1)} %collective-permute-done.3.a1), channel_id=1, source_target_pairs={{0,1},{1,0},{8,9},{9,8},{16,17},{17,16},{24,25},{25,24},{128,129},... | collective-permute-start | bytes 1769480 | tf_op jit(solution)/shard_map/ppermute | solution.py:218
  45.6 2.9 %collective-permute-start.6 = (bf16[32,72,128]{2,1,0:T(8,128)(2,1)S(1)}, bf16[32,72,128]{2,1,0:T(8,128)(2,1)S(1)}, u32[]{:S(2)}, u32[]{:S(2)}) collective-permute-start(bf16[32,72,128]{2,1,0:T(8,128)(2,1)S(1)} %collective-permute-done.5.a2), channel_id=1, source_target_pairs={{0,1},{1,0},{8,9},{9,8},{16,17},{17,16},{24,25},{25,24},{128,129},... | collective-permute-start | bytes 1769480 | tf_op jit(solution)/shard_map/ppermute | solution.py:218
  45.7 3.3 %collective-permute-start.8 = (bf16[32,72,128]{2,1,0:T(8,128)(2,1)S(1)}, bf16[32,72,128]{2,1,0:T(8,128)(2,1)S(1)}, u32[]{:S(2)}, u32[]{:S(2)}) collective-permute-start(bf16[32,72,128]{2,1,0:T(8,128)(2,1)S(1)} %collective-permute-done.7.a3), channel_id=1, source_target_pairs={{0,1},{1,0},{8,9},{9,8},{16,17},{17,16},{24,25},{25,24},{128,129},... | collective-permute-start | bytes 1769480 | tf_op jit(solution)/shard_map/ppermute | solution.py:218

commit v5 on v4

--- a/solution.py
+++ b/solution.py
@@ -158,11 +158,13 @@
         store(i).wait()
 
 
-def merge(scalars, lists, near, shape, out=None):
+def merge(scalars, lists, near, shape, token, out=None):
     inside = pl.BlockSpec(memory_space=pltpu.VMEM)
     outside = pl.BlockSpec(memory_space=pl.ANY)
     args = [scalars, *lists, near]
     in_specs = [pl.BlockSpec(memory_space=pltpu.SMEM)] + [inside] * (len(args) - 1)
+    args.append(token)
+    in_specs.append(outside)
     aliases = {}
     if out is not None:
         aliases = {len(args): 0}
@@ -214,11 +216,12 @@
         own = own.reshape(32, ROWS, 128)
         near, token = fetch(own, weight)
         lists = [lax.ppermute(own, AXES, from_neighbour(a)) for a in range(3)]
-        lists = [own] + [lax.optimization_barrier((token, a))[1] for a in lists]
-        swapped = [lax.ppermute(a, AXES, other_core()) for a in lists]
-
-        out = merge(here, lists, near, weight.shape)
-        return merge(there, swapped, near, weight.shape, out)
+        token, own_after = lax.optimization_barrier((token, own))
+        lists = [own] + lists
+        swapped = [lax.ppermute(a, AXES, other_core()) for a in (own_after, *lists[1:])]
+
+        out = merge(here, lists, near, weight.shape, token)
+        return merge(there, swapped, near, weight.shape, token, out)
 
     spec = P(None, None, "tp", None)
     return jax.shard_map(

time: 51.6 us -> 50.7 us (0.983)
  waiting for transfers between devices: 7.66 us -> 5.05 us
  starting transfers between devices: 18.2 us -> 20.5 us
  Pallas kernels: 7.51 us -> 6.91 us
    ppermute x4, starting transfers between devices: 5.67 us -> 7.95 us  [local(): lax.ppermute(a, AXES, other_core())]
    ppermute x3, waiting for transfers between devices: 3.56 us -> 1.35 us  [local(): lists = [lax.ppermute(own, AXES, from_neighbour(a)) for a in range(3)]]
    pallas_call x1, Pallas kernels: 2.81 us -> 2.22 us  [fetch(): pl.pallas_call(fetch_kernel, in_specs=[outside] * 2, out_specs=[inside] *...]
  transfers between devices with their start and end apart: 9 -> 9, of which waited for: 6 -> 3; matrix products, arithmetic and copies ran while one was open for 0% -> 0% of each run, Pallas kernels for 10% -> 9%
where the time goes in v5:
time: 50.7 us; the launch traced here: 50.4 us
  starting transfers between devices  20.5 us (40%)
  blocking collectives  16.7 us (33%)
  Pallas kernels  6.91 us (14%)
  waiting for transfers between devices  5.05 us (10%)
  local copies, waits for them, and re-layouts  1 us (2%)
    all_to_all x1, blocking collectives, local(): own = lax.all_to_all(many, AXES, 0, 0, axis_index_groups=groups, tiled=True)  16.7 us
    ppermute x2, starting transfers between devices, local(): lax.ppermute(column, AXES, along_z(flip))  8.05 us
    ppermute x4, starting transfers between devices, local(): lax.ppermute(a, AXES, other_core())  7.95 us
    pallas_call x2, Pallas kernels, merge(): pl.pallas_call(merge_kernel, in_specs=in_specs, out_specs=outside, out_sh...  4.69 us
    ppermute x3, starting transfers between devices, local(): lists = [lax.ppermute(own, AXES, from_neighbour(a)) for a in range(3)]  4.49 us
    ppermute x2, waiting for transfers between devices, local(): lax.ppermute(column, AXES, along_z(flip))  3.69 us
    pallas_call x1, Pallas kernels, fetch(): pl.pallas_call(fetch_kernel, in_specs=[outside] * 2, out_specs=[inside] *...  2.22 us
    ppermute x3, waiting for transfers between devices, local(): lists = [lax.ppermute(own, AXES, from_neighbour(a)) for a in range(3)]  1.35 us
  transfers between devices with their start and end apart: 9, of which 3 were waited for; matrix products, arithmetic and copies ran while one was open for 0% of the time, Pallas kernels for 9%

profile of v5, /device:TPU:1, one launch (start us, length us, event | category | flops | bytes accessed | tf_op | source)
XLA Modules:
  0.0 50.4 jit_solution(17672075657872279236)
XLA Ops:
  0.0 0.0 copy-start
  0.0 0.7 %dynamic-slice_bitcast_fusion = bf16[8,2,64]{2,0,1:T(8,128)(2,1)S(1)} fusion(bf16[2,2,8,64]{3,2,1,0:T(8,128)(2,1)} %param.4, s32[]{:T(128)S(6)} %select_n.24), kind=kLoop, calls=%fused_computation.3 | loop fusion | bytes 4100 | tf_op jit(solution)/shard_map/transpose | solution.py:204
  0.7 0.1 reshape.12
  0.8 0.0 copy-done
  0.8 0.1 copy.8
  1.0 0.1 add_add_fusion
  1.1 6.9 %collective-permute-start = (bf16[1,72,128]{2,1,0:T(8,128)(2,1)S(1)}, bf16[1,72,128]{2,1,0:T(8,128)(2,1)S(1)}, u32[]{:S(2)}, u32[]{:S(2)}) collective-permute-start(bf16[1,72,128]{2,1,0:T(8,128)(2,1)S(1)} %bitcast.19), channel_id=1, source_target_pairs={{0,144},{1,145},{8,152},{9,153},{16,128},{17,129},{24,136},{25,137... | collective-permute-start | bytes 55304 | tf_op jit(solution)/shard_map/ppermute | solution.py:213
  7.9 1.2 %collective-permute-done = bf16[1,72,128]{2,1,0:T(8,128)(2,1)S(1)} collective-permute-done((bf16[1,72,128]{2,1,0:T(8,128)(2,1)S(1)}, bf16[1,72,128]{2,1,0:T(8,128)(2,1)S(1)}, u32[]{:S(2)}, u32[]{:S(2)}) %collective-permute-start) | collective-permute-done | bytes 18464 | tf_op jit(solution)/shard_map/ppermute | solution.py:213
  9.1 1.2 %collective-permute-start.1 = (bf16[2,72,128]{2,1,0:T(8,128)(2,1)S(1)}, bf16[2,72,128]{2,1,0:T(8,128)(2,1)S(1)}, u32[]{:S(2)}, u32[]{:S(2)}) collective-permute-start(bf16[2,72,128]{2,1,0:T(8,128)(2,1)S(1)} %pad_maximum_fusion.1), channel_id=1, source_target_pairs={{0,16},{1,17},{8,24},{9,25},{16,0},{17,1},{24,8},{25,9},{128,144},... | collective-permute-start | bytes 110600 | tf_op jit(solution)/shard_map/ppermute | solution.py:213
  10.3 2.5 %collective-permute-done.1 = bf16[2,72,128]{2,1,0:T(8,128)(2,1)S(1)} collective-permute-done((bf16[2,72,128]{2,1,0:T(8,128)(2,1)S(1)}, bf16[2,72,128]{2,1,0:T(8,128)(2,1)S(1)}, u32[]{:S(2)}, u32[]{:S(2)}) %collective-permute-start.1) | collective-permute-done | bytes 36896 | tf_op jit(solution)/shard_map/ppermute | solution.py:213
  12.8 0.1 broadcast_in_dim.10
  12.9 16.7 %all_to_all.5 = bf16[8,4,72,128]{3,2,1,0:T(8,128)(2,1)S(1)} all-to-all(bf16[8,4,72,128]{3,2,1,0:T(8,128)(2,1)S(1)} %broadcast_in_dim.10), channel_id=1, replica_groups={{0,42,64,106,4,46,68,110},{1,43,65,107,5,47,69,111},{34,8,98,72,38,12,1..., dimensions={0} | all-to-all | bytes 1179648 | tf_op jit(solution)/shard_map/all_to_all | solution.py:215
  29.6 2.7 %collective-permute-start.7 = (bf16[32,72,128]{2,1,0:T(8,128)(2,1)S(1)}, bf16[32,72,128]{2,1,0:T(8,128)(2,1)S(1)}, u32[]{:S(2)}, u32[]{:S(2)}) collective-permute-start(bf16[32,72,128]{2,1,0:T(8,128)(2,1)S(1)} %bitcast.13), channel_id=1, source_target_pairs={{0,8},{1,153},{8,16},{9,1},{16,24},{17,9},{24,128},{25,17},{128,13... | collective-permute-start | bytes 1769480 | tf_op jit(solution)/shard_map/ppermute | solution.py:218
  32.3 0.5 collective-permute-start.5
  32.8 1.3 %collective-permute-start.3 = (bf16[32,72,128]{2,1,0:T(8,128)(2,1)S(1)}, bf16[32,72,128]{2,1,0:T(8,128)(2,1)S(1)}, u32[]{:S(2)}, u32[]{:S(2)}) collective-permute-start(bf16[32,72,128]{2,1,0:T(8,128)(2,1)S(1)} %bitcast.15), channel_id=1, source_target_pairs={{0,2},{1,7},{8,10},{9,15},{16,18},{17,23},{24,26},{25,31},{128,130... | collective-permute-start | bytes 1769480 | tf_op jit(solution)/shard_map/ppermute | solution.py:218
  34.1 2.2 %shard_map.37 = (bf16[2,4,2,64,2048]{4,3,2,1,0:T(8,128)(2,1)S(1)}, f32[8,128]{1,0:T(8,128)S(1)}) custom-call(bf16[32,72,128]{2,1,0:T(8,128)(2,1)S(1)} %bitcast.16, bf16[2,2,64,8192]{3,2,1,0:T(8,128)(2,1)} %w_ref.1), custom_call_target="tpu_custom_call" | custom-call | bytes 8388608 | tf_op jit(solution)/shard_map/pallas_call | solution.py:85
  36.3 1.5 %collective-permute-start.2 = (bf16[32,72,128]{2,1,0:T(8,128)(2,1)S(1)}, bf16[32,72,128]{2,1,0:T(8,128)(2,1)S(1)}, u32[]{:S(2)}, u32[]{:S(2)}) collective-permute-start(bf16[32,72,128]{2,1,0:T(8,128)(2,1)S(1)} %bitcast.17), channel_id=1, source_target_pairs={{0,1},{1,0},{8,9},{9,8},{16,17},{17,16},{24,25},{25,24},{128,129},... | collective-permute-start | bytes 1769480 | tf_op jit(solution)/shard_map/ppermute | solution.py:221
  37.8 1.3 %collective-permute-done.7.a3 = bf16[32,72,128]{2,1,0:T(8,128)(2,1)S(1)} collective-permute-done((bf16[32,72,128]{2,1,0:T(8,128)(2,1)S(1)}, bf16[32,72,128]{2,1,0:T(8,128)(2,1)S(1)}, u32[]{:S(2)}, u32[]{:S(2)}) %collective-permute-start.7) | collective-permute-done | bytes 589856 | tf_op jit(solution)/shard_map/ppermute | solution.py:218
  39.2 5.4 %collective-permute-start.8 = (bf16[32,72,128]{2,1,0:T(8,128)(2,1)S(1)}, bf16[32,72,128]{2,1,0:T(8,128)(2,1)S(1)}, u32[]{:S(2)}, u32[]{:S(2)}) collective-permute-start(bf16[32,72,128]{2,1,0:T(8,128)(2,1)S(1)} %collective-permute-done.7.a3), channel_id=1, source_target_pairs={{0,1},{1,0},{8,9},{9,8},{16,17},{17,16},{24,25},{25,24},{128,129},... | collective-permute-start | bytes 1769480 | tf_op jit(solution)/shard_map/ppermute | solution.py:221
  44.6 0.0 collective-permute-done.5.a2
  44.6 0.5 %collective-permute-start.6 = (bf16[32,72,128]{2,1,0:T(8,128)(2,1)S(1)}, bf16[32,72,128]{2,1,0:T(8,128)(2,1)S(1)}, u32[]{:S(2)}, u32[]{:S(2)}) collective-permute-start(bf16[32,72,128]{2,1,0:T(8,128)(2,1)S(1)} %collective-permute-done.5.a2), channel_id=1, source_target_pairs={{0,1},{1,0},{8,9},{9,8},{16,17},{17,16},{24,25},{25,24},{128,129},... | collective-permute-start | bytes 1769480 | tf_op jit(solution)/shard_map/ppermute | solution.py:221
  45.1 0.0 collective-permute-done.3.a1
  45.1 0.6 %collective-permute-start.4 = (bf16[32,72,128]{2,1,0:T(8,128)(2,1)S(1)}, bf16[32,72,128]{2,1,0:T(8,128)(2,1)S(1)}, u32[]{:S(2)}, u32[]{:S(2)}) collective-permute-start(bf16[32,72,128]{2,1,0:T(8,128)(2,1)S(1)} %collective-permute-done.3.a1), channel_id=1, source_target_pairs={{0,1},{1,0},{8,9},{9,8},{16,17},{17,16},{24,25},{25,24},{128,129},... | collective-permute-start | bytes 1769480 | tf_op jit(solution)/shard_map/ppermute | solution.py:221
  45.6 2.3 %shard_map.38.rest_1_ = bf16[2,2,64,8192]{3,2,1,0:T(8,128)(2,1)} custom-call(s32[4]{0:T(128)S(1)} %get-tuple-element.18.s_ref, bf16[32,72,128]{2,1,0:T(8,128)(2,1)S(1)} %bitcast.18, bf16[32,72,128]{2,1,0:T(8,128)(2,1)S(1)} %collective-permute-done.3.a1, bf16[32,72,128]{2,1,0:T(8,128)(2,1)S(1)} %collective-permute-done.5.a2, ...), custom_call_target="tpu_custom_call" | custom-call | flops 268435456 | bytes 6291456 | tf_op jit(solution)/shard_map/pallas_call | solution.py:173
  48.0 0.0 collective-permute-done.2.a0
  48.0 0.0 collective-permute-done.8.a3
  48.0 0.0 collective-permute-done.6.a2
  48.0 0.0 collective-permute-done.4.a1
  48.0 2.3 %shard_map.39 = bf16[2,2,64,8192]{3,2,1,0:T(8,128)(2,1)} custom-call(s32[4]{0:T(128)S(1)} %get-tuple-element.12.s_ref, bf16[32,72,128]{2,1,0:T(8,128)(2,1)S(1)} %collective-permute-done.2.a0, bf16[32,72,128]{2,1,0:T(8,128)(2,1)S(1)} %collective-permute-done.4.a1, bf16[32,72,128]{2,1,0:T(8,128)(2,1)S(1)} %collective-permute-done.6.a2, ...), custom_call_target="tpu_custom_call", output_to_operand_aliasing={{}: (7, {})} | custom-call | flops 268435456 | bytes 6291456 | tf_op jit(solution)/shard_map/pallas_call | solution.py:173
  (5 shorter events, 0.0 us)
Async XLA Ops:
  0.0 0.8 %copy-start = (bf16[2,2,64,64]{3,2,1,0:T(8,128)(2,1)S(1)}, bf16[2,2,64,64]{3,2,1,0:T(8,128)(2,1)}, u32[]{:S(2)}) copy-start(bf16[2,2,64,64]{3,2,1,0:T(8,128)(2,1)} %param.3) | copy-start | bytes 98308
  1.1 8.0 %collective-permute-start = (bf16[1,72,128]{2,1,0:T(8,128)(2,1)S(1)}, bf16[1,72,128]{2,1,0:T(8,128)(2,1)S(1)}, u32[]{:S(2)}, u32[]{:S(2)}) collective-permute-start(bf16[1,72,128]{2,1,0:T(8,128)(2,1)S(1)} %bitcast.19), channel_id=1, source_target_pairs={{0,144},{1,145},{8,152},{9,153},{16,128},{17,129},{24,136},{25,137... | collective-permute-start | bytes 55304 | tf_op jit(solution)/shard_map/ppermute | solution.py:213
  9.1 3.7 %collective-permute-start.1 = (bf16[2,72,128]{2,1,0:T(8,128)(2,1)S(1)}, bf16[2,72,128]{2,1,0:T(8,128)(2,1)S(1)}, u32[]{:S(2)}, u32[]{:S(2)}) collective-permute-start(bf16[2,72,128]{2,1,0:T(8,128)(2,1)S(1)} %pad_maximum_fusion.1), channel_id=1, source_target_pairs={{0,16},{1,17},{8,24},{9,25},{16,0},{17,1},{24,8},{25,9},{128,144},... | collective-permute-start | bytes 110600 | tf_op jit(solution)/shard_map/ppermute | solution.py:213
  29.6 9.5 %collective-permute-start.7 = (bf16[32,72,128]{2,1,0:T(8,128)(2,1)S(1)}, bf16[32,72,128]{2,1,0:T(8,128)(2,1)S(1)}, u32[]{:S(2)}, u32[]{:S(2)}) collective-permute-start(bf16[32,72,128]{2,1,0:T(8,128)(2,1)S(1)} %bitcast.13), channel_id=1, source_target_pairs={{0,8},{1,153},{8,16},{9,1},{16,24},{17,9},{24,128},{25,17},{128,13... | collective-permute-start | bytes 1769480 | tf_op jit(solution)/shard_map/ppermute | solution.py:218
  32.3 12.2 %collective-permute-start.5 = (bf16[32,72,128]{2,1,0:T(8,128)(2,1)S(1)}, bf16[32,72,128]{2,1,0:T(8,128)(2,1)S(1)}, u32[]{:S(2)}, u32[]{:S(2)}) collective-permute-start(bf16[32,72,128]{2,1,0:T(8,128)(2,1)S(1)} %bitcast.14), channel_id=1, source_target_pairs={{0,32},{1,97},{8,40},{9,105},{16,48},{17,113},{24,56},{25,121},{12... | collective-permute-start | bytes 1769480 | tf_op jit(solution)/shard_map/ppermute | solution.py:218
  32.8 12.3 %collective-permute-start.3 = (bf16[32,72,128]{2,1,0:T(8,128)(2,1)S(1)}, bf16[32,72,128]{2,1,0:T(8,128)(2,1)S(1)}, u32[]{:S(2)}, u32[]{:S(2)}) collective-permute-start(bf16[32,72,128]{2,1,0:T(8,128)(2,1)S(1)} %bitcast.15), channel_id=1, source_target_pairs={{0,2},{1,7},{8,10},{9,15},{16,18},{17,23},{24,26},{25,31},{128,130... | collective-permute-start | bytes 1769480 | tf_op jit(solution)/shard_map/ppermute | solution.py:218
  36.3 11.7 %collective-permute-start.2 = (bf16[32,72,128]{2,1,0:T(8,128)(2,1)S(1)}, bf16[32,72,128]{2,1,0:T(8,128)(2,1)S(1)}, u32[]{:S(2)}, u32[]{:S(2)}) collective-permute-start(bf16[32,72,128]{2,1,0:T(8,128)(2,1)S(1)} %bitcast.17), channel_id=1, source_target_pairs={{0,1},{1,0},{8,9},{9,8},{16,17},{17,16},{24,25},{25,24},{128,129},... | collective-permute-start | bytes 1769480 | tf_op jit(solution)/shard_map/ppermute | solution.py:221
  39.2 8.8 %collective-permute-start.8 = (bf16[32,72,128]{2,1,0:T(8,128)(2,1)S(1)}, bf16[32,72,128]{2,1,0:T(8,128)(2,1)S(1)}, u32[]{:S(2)}, u32[]{:S(2)}) collective-permute-start(bf16[32,72,128]{2,1,0:T(8,128)(2,1)S(1)} %collective-permute-done.7.a3), channel_id=1, source_target_pairs={{0,1},{1,0},{8,9},{9,8},{16,17},{17,16},{24,25},{25,24},{128,129},... | collective-permute-start | bytes 1769480 | tf_op jit(solution)/shard_map/ppermute | solution.py:221
  44.6 3.4 %collective-permute-start.6 = (bf16[32,72,128]{2,1,0:T(8,128)(2,1)S(1)}, bf16[32,72,128]{2,1,0:T(8,128)(2,1)S(1)}, u32[]{:S(2)}, u32[]{:S(2)}) collective-permute-start(bf16[32,72,128]{2,1,0:T(8,128)(2,1)S(1)} %collective-permute-done.5.a2), channel_id=1, source_target_pairs={{0,1},{1,0},{8,9},{9,8},{16,17},{17,16},{24,25},{25,24},{128,129},... | collective-permute-start | bytes 1769480 | tf_op jit(solution)/shard_map/ppermute | solution.py:221
  45.1 2.9 %collective-permute-start.4 = (bf16[32,72,128]{2,1,0:T(8,128)(2,1)S(1)}, bf16[32,72,128]{2,1,0:T(8,128)(2,1)S(1)}, u32[]{:S(2)}, u32[]{:S(2)}) collective-permute-start(bf16[32,72,128]{2,1,0:T(8,128)(2,1)S(1)} %collective-permute-done.3.a1), channel_id=1, source_target_pairs={{0,1},{1,0},{8,9},{9,8},{16,17},{17,16},{24,25},{25,24},{128,129},... | collective-permute-start | bytes 1769480 | tf_op jit(solution)/shard_map/ppermute | solution.py:221

commit v6 on v5

--- a/solution.py
+++ b/solution.py
@@ -53,7 +53,7 @@
     pairs = []
     for x, y, z, c in coords():
         q = [x, y, z]
-        q[axis] += 1 if c == 0 else -1
+        q[axis] += 1 if c == (axis in (0, 1)) else -1
         pairs.append((linear(x, y, z, c), linear(q[0] % NX, q[1] % NY, q[2] % NZ, c)))
     return pairs
 
@@ -124,8 +124,13 @@
     c = lax.broadcasted_iota(jnp.int32, u.shape, 1) // 64
     u_ref[...] = jnp.where(r == c, u, 0.0).astype(jnp.bfloat16)
 
-    def store(i):
-        return pltpu.make_async_copy(buf.at[i], part(o_ref, layer, i), sem.at[i])
+    def store(i, y0):
+        column = i * CHUNK + y0 * (CHUNK // 2)
+        return pltpu.make_async_copy(
+            buf.at[i, :, :, pl.ds(y0 * (CHUNK // 2), CHUNK // 2)],
+            o_ref.at[layer, :, :, pl.ds(column, CHUNK // 2)],
+            sem.at[2 * i + y0],
+        )
 
     for i in range(CHUNKS):
         u = u_ref[...]
@@ -153,9 +158,10 @@
                     for p in range(2):
                         w = w_ref[layer, i, p, :, at].astype(jnp.float32)
                         buf[i, p, :, at] = (w + delta[p * 64 : p * 64 + 64]).astype(jnp.bfloat16)
-        store(i).start()
+            store(i, y0).start()
     for i in range(CHUNKS):
-        store(i).wait()
+        for y0 in range(2):
+            store(i, y0).wait()
 
 
 def merge(scalars, lists, near, shape, token, out=None):
@@ -178,7 +184,7 @@
         scratch_shapes=[
             pltpu.VMEM((CHUNKS, 2, 64, CHUNK), jnp.bfloat16),
             pltpu.VMEM((128, 128), jnp.bfloat16),
-            pltpu.SemaphoreType.DMA((CHUNKS,)),
+            pltpu.SemaphoreType.DMA((2 * CHUNKS,)),
         ],
         input_output_aliases=aliases,
         compiler_params=pltpu.CompilerParams(vmem_limit_bytes=VMEM_LIMIT),

time: 50.7 us -> 50.4 us (level)
    ppermute x3, starting transfers between devices: 4.49 us -> 3.29 us  [local(): lists = [lax.ppermute(own, AXES, from_neighbour(a)) for a in range(3)]]
    ppermute x4, starting transfers between devices: 7.95 us -> 9.02 us  [local(): lax.ppermute(a, AXES, other_core())]
  transfers between devices with their start and end apart: 9 -> 9, of which waited for: 3 -> 4; matrix products, arithmetic and copies ran while one was open for 0% -> 0% of each run, Pallas kernels for 9% -> 9%
where the time goes in v6:
time: 50.4 us; the launch traced here: 50.2 us
  starting transfers between devices  20.4 us (40%)
  blocking collectives  16.7 us (33%)
  Pallas kernels  6.82 us (14%)
  waiting for transfers between devices  5.07 us (10%)
  local copies, waits for them, and re-layouts  1 us (2%)
    all_to_all x1, blocking collectives, local(): own = lax.all_to_all(many, AXES, 0, 0, axis_index_groups=groups, tiled=True)  16.7 us
    ppermute x4, starting transfers between devices, local(): lax.ppermute(a, AXES, other_core())  9.02 us
    ppermute x2, starting transfers between devices, local(): lax.ppermute(column, AXES, along_z(flip))  8.05 us
    pallas_call x2, Pallas kernels, merge(): pl.pallas_call(merge_kernel, in_specs=in_specs, out_specs=outside, out_sh...  4.6 us
    ppermute x2, waiting for transfers between devices, local(): lax.ppermute(column, AXES, along_z(flip))  3.69 us
    ppermute x3, starting transfers between devices, local(): lists = [lax.ppermute(own, AXES, from_neighbour(a)) for a in range(3)]  3.29 us
    pallas_call x1, Pallas kernels, fetch(): pl.pallas_call(fetch_kernel, in_specs=[outside] * 2, out_specs=[inside] *...  2.22 us
  transfers between devices with their start and end apart: 9, of which 4 were waited for; matrix products, arithmetic and copies ran while one was open for 0% of the time, Pallas kernels for 9%

profile of v6, /device:TPU:1, one launch (start us, length us, event | category | flops | bytes accessed | tf_op | source)
XLA Modules:
  0.0 50.2 jit_solution(3536833349430059667)
XLA Ops:
  0.0 0.0 copy-start
  0.0 0.7 %dynamic-slice_bitcast_fusion = bf16[8,2,64]{2,0,1:T(8,128)(2,1)S(1)} fusion(bf16[2,2,8,64]{3,2,1,0:T(8,128)(2,1)} %param.4, s32[]{:T(128)S(6)} %select_n.24), kind=kLoop, calls=%fused_computation.3 | loop fusion | bytes 4100 | tf_op jit(solution)/shard_map/transpose | solution.py:210
  0.7 0.1 reshape.12
  0.8 0.0 copy-done
  0.8 0.1 copy.8
  1.0 0.1 add_add_fusion
  1.1 6.9 %collective-permute-start = (bf16[1,72,128]{2,1,0:T(8,128)(2,1)S(1)}, bf16[1,72,128]{2,1,0:T(8,128)(2,1)S(1)}, u32[]{:S(2)}, u32[]{:S(2)}) collective-permute-start(bf16[1,72,128]{2,1,0:T(8,128)(2,1)S(1)} %bitcast.19), channel_id=1, source_target_pairs={{0,144},{1,145},{8,152},{9,153},{16,128},{17,129},{24,136},{25,137... | collective-permute-start | bytes 55304 | tf_op jit(solution)/shard_map/ppermute | solution.py:219
  7.9 1.2 %collective-permute-done = bf16[1,72,128]{2,1,0:T(8,128)(2,1)S(1)} collective-permute-done((bf16[1,72,128]{2,1,0:T(8,128)(2,1)S(1)}, bf16[1,72,128]{2,1,0:T(8,128)(2,1)S(1)}, u32[]{:S(2)}, u32[]{:S(2)}) %collective-permute-start) | collective-permute-done | bytes 18464 | tf_op jit(solution)/shard_map/ppermute | solution.py:219
  9.1 1.2 %collective-permute-start.1 = (bf16[2,72,128]{2,1,0:T(8,128)(2,1)S(1)}, bf16[2,72,128]{2,1,0:T(8,128)(2,1)S(1)}, u32[]{:S(2)}, u32[]{:S(2)}) collective-permute-start(bf16[2,72,128]{2,1,0:T(8,128)(2,1)S(1)} %pad_maximum_fusion.1), channel_id=1, source_target_pairs={{0,16},{1,17},{8,24},{9,25},{16,0},{17,1},{24,8},{25,9},{128,144},... | collective-permute-start | bytes 110600 | tf_op jit(solution)/shard_map/ppermute | solution.py:219
  10.3 2.5 %collective-permute-done.1 = bf16[2,72,128]{2,1,0:T(8,128)(2,1)S(1)} collective-permute-done((bf16[2,72,128]{2,1,0:T(8,128)(2,1)S(1)}, bf16[2,72,128]{2,1,0:T(8,128)(2,1)S(1)}, u32[]{:S(2)}, u32[]{:S(2)}) %collective-permute-start.1) | collective-permute-done | bytes 36896 | tf_op jit(solution)/shard_map/ppermute | solution.py:219
  12.8 0.1 broadcast_in_dim.10
  12.9 16.7 %all_to_all.5 = bf16[8,4,72,128]{3,2,1,0:T(8,128)(2,1)S(1)} all-to-all(bf16[8,4,72,128]{3,2,1,0:T(8,128)(2,1)S(1)} %broadcast_in_dim.10), channel_id=1, replica_groups={{0,42,64,106,4,46,68,110},{1,43,65,107,5,47,69,111},{34,8,98,72,38,12,1..., dimensions={0} | all-to-all | bytes 1179648 | tf_op jit(solution)/shard_map/all_to_all | solution.py:221
  29.6 2.7 %collective-permute-start.7 = (bf16[32,72,128]{2,1,0:T(8,128)(2,1)S(1)}, bf16[32,72,128]{2,1,0:T(8,128)(2,1)S(1)}, u32[]{:S(2)}, u32[]{:S(2)}) collective-permute-start(bf16[32,72,128]{2,1,0:T(8,128)(2,1)S(1)} %bitcast.13), channel_id=1, source_target_pairs={{0,8},{1,153},{8,16},{9,1},{16,24},{17,9},{24,128},{25,17},{128,13... | collective-permute-start | bytes 1769480 | tf_op jit(solution)/shard_map/ppermute | solution.py:224
  32.3 0.0 collective-permute-start.5
  32.3 0.6 %collective-permute-start.3 = (bf16[32,72,128]{2,1,0:T(8,128)(2,1)S(1)}, bf16[32,72,128]{2,1,0:T(8,128)(2,1)S(1)}, u32[]{:S(2)}, u32[]{:S(2)}) collective-permute-start(bf16[32,72,128]{2,1,0:T(8,128)(2,1)S(1)} %bitcast.15), channel_id=1, source_target_pairs={{0,6},{1,3},{8,14},{9,11},{16,22},{17,19},{24,30},{25,27},{128,134... | collective-permute-start | bytes 1769480 | tf_op jit(solution)/shard_map/ppermute | solution.py:224
  32.9 2.2 %shard_map.37 = (bf16[2,4,2,64,2048]{4,3,2,1,0:T(8,128)(2,1)S(1)}, f32[8,128]{1,0:T(8,128)S(1)}) custom-call(bf16[32,72,128]{2,1,0:T(8,128)(2,1)S(1)} %bitcast.16, bf16[2,2,64,8192]{3,2,1,0:T(8,128)(2,1)} %w_ref.1), custom_call_target="tpu_custom_call" | custom-call | bytes 8388608 | tf_op jit(solution)/shard_map/pallas_call | solution.py:85
  35.1 3.1 %collective-permute-start.2 = (bf16[32,72,128]{2,1,0:T(8,128)(2,1)S(1)}, bf16[32,72,128]{2,1,0:T(8,128)(2,1)S(1)}, u32[]{:S(2)}, u32[]{:S(2)}) collective-permute-start(bf16[32,72,128]{2,1,0:T(8,128)(2,1)S(1)} %bitcast.17), channel_id=1, source_target_pairs={{0,1},{1,0},{8,9},{9,8},{16,17},{17,16},{24,25},{25,24},{128,129},... | collective-permute-start | bytes 1769480 | tf_op jit(solution)/shard_map/ppermute | solution.py:227
  38.3 0.9 %collective-permute-done.7.a3 = bf16[32,72,128]{2,1,0:T(8,128)(2,1)S(1)} collective-permute-done((bf16[32,72,128]{2,1,0:T(8,128)(2,1)S(1)}, bf16[32,72,128]{2,1,0:T(8,128)(2,1)S(1)}, u32[]{:S(2)}, u32[]{:S(2)}) %collective-permute-start.7) | collective-permute-done | bytes 589856 | tf_op jit(solution)/shard_map/ppermute | solution.py:224
  39.2 5.4 %collective-permute-start.8 = (bf16[32,72,128]{2,1,0:T(8,128)(2,1)S(1)}, bf16[32,72,128]{2,1,0:T(8,128)(2,1)S(1)}, u32[]{:S(2)}, u32[]{:S(2)}) collective-permute-start(bf16[32,72,128]{2,1,0:T(8,128)(2,1)S(1)} %collective-permute-done.7.a3), channel_id=1, source_target_pairs={{0,1},{1,0},{8,9},{9,8},{16,17},{17,16},{24,25},{25,24},{128,129},... | collective-permute-start | bytes 1769480 | tf_op jit(solution)/shard_map/ppermute | solution.py:227
  44.6 0.0 collective-permute-done.5.a2
  44.6 0.0 collective-permute-start.6
  44.6 0.0 collective-permute-done.3.a1
  44.6 0.5 %collective-permute-start.4 = (bf16[32,72,128]{2,1,0:T(8,128)(2,1)S(1)}, bf16[32,72,128]{2,1,0:T(8,128)(2,1)S(1)}, u32[]{:S(2)}, u32[]{:S(2)}) collective-permute-start(bf16[32,72,128]{2,1,0:T(8,128)(2,1)S(1)} %collective-permute-done.3.a1), channel_id=1, source_target_pairs={{0,1},{1,0},{8,9},{9,8},{16,17},{17,16},{24,25},{25,24},{128,129},... | collective-permute-start | bytes 1769480 | tf_op jit(solution)/shard_map/ppermute | solution.py:227
  45.1 2.3 %shard_map.38.rest_1_ = bf16[2,2,64,8192]{3,2,1,0:T(8,128)(2,1)} custom-call(s32[4]{0:T(128)S(1)} %get-tuple-element.18.s_ref, bf16[32,72,128]{2,1,0:T(8,128)(2,1)S(1)} %bitcast.18, bf16[32,72,128]{2,1,0:T(8,128)(2,1)S(1)} %collective-permute-done.3.a1, bf16[32,72,128]{2,1,0:T(8,128)(2,1)S(1)} %collective-permute-done.5.a2, ...), custom_call_target="tpu_custom_call" | custom-call | flops 268435456 | bytes 6291456 | tf_op jit(solution)/shard_map/pallas_call | solution.py:179
  47.4 0.0 collective-permute-done.2.a0
  47.4 0.0 collective-permute-done.8.a3
  47.4 0.0 collective-permute-done.6.a2
  47.4 0.5 collective-permute-done.4.a1
  47.9 2.3 %shard_map.39 = bf16[2,2,64,8192]{3,2,1,0:T(8,128)(2,1)} custom-call(s32[4]{0:T(128)S(1)} %get-tuple-element.12.s_ref, bf16[32,72,128]{2,1,0:T(8,128)(2,1)S(1)} %collective-permute-done.2.a0, bf16[32,72,128]{2,1,0:T(8,128)(2,1)S(1)} %collective-permute-done.4.a1, bf16[32,72,128]{2,1,0:T(8,128)(2,1)S(1)} %collective-permute-done.6.a2, ...), custom_call_target="tpu_custom_call", output_to_operand_aliasing={{}: (7, {})} | custom-call | flops 268435456 | bytes 6291456 | tf_op jit(solution)/shard_map/pallas_call | solution.py:179
  (5 shorter events, 0.0 us)
Async XLA Ops:
  0.0 0.8 %copy-start = (bf16[2,2,64,64]{3,2,1,0:T(8,128)(2,1)S(1)}, bf16[2,2,64,64]{3,2,1,0:T(8,128)(2,1)}, u32[]{:S(2)}) copy-start(bf16[2,2,64,64]{3,2,1,0:T(8,128)(2,1)} %param.3) | copy-start | bytes 98308
  1.1 8.0 %collective-permute-start = (bf16[1,72,128]{2,1,0:T(8,128)(2,1)S(1)}, bf16[1,72,128]{2,1,0:T(8,128)(2,1)S(1)}, u32[]{:S(2)}, u32[]{:S(2)}) collective-permute-start(bf16[1,72,128]{2,1,0:T(8,128)(2,1)S(1)} %bitcast.19), channel_id=1, source_target_pairs={{0,144},{1,145},{8,152},{9,153},{16,128},{17,129},{24,136},{25,137... | collective-permute-start | bytes 55304 | tf_op jit(solution)/shard_map/ppermute | solution.py:219
  9.1 3.7 %collective-permute-start.1 = (bf16[2,72,128]{2,1,0:T(8,128)(2,1)S(1)}, bf16[2,72,128]{2,1,0:T(8,128)(2,1)S(1)}, u32[]{:S(2)}, u32[]{:S(2)}) collective-permute-start(bf16[2,72,128]{2,1,0:T(8,128)(2,1)S(1)} %pad_maximum_fusion.1), channel_id=1, source_target_pairs={{0,16},{1,17},{8,24},{9,25},{16,0},{17,1},{24,8},{25,9},{128,144},... | collective-permute-start | bytes 110600 | tf_op jit(solution)/shard_map/ppermute | solution.py:219
  29.6 9.5 %collective-permute-start.7 = (bf16[32,72,128]{2,1,0:T(8,128)(2,1)S(1)}, bf16[32,72,128]{2,1,0:T(8,128)(2,1)S(1)}, u32[]{:S(2)}, u32[]{:S(2)}) collective-permute-start(bf16[32,72,128]{2,1,0:T(8,128)(2,1)S(1)} %bitcast.13), channel_id=1, source_target_pairs={{0,8},{1,153},{8,16},{9,1},{16,24},{17,9},{24,128},{25,17},{128,13... | collective-permute-start | bytes 1769480 | tf_op jit(solution)/shard_map/ppermute | solution.py:224
  32.3 12.2 %collective-permute-start.5 = (bf16[32,72,128]{2,1,0:T(8,128)(2,1)S(1)}, bf16[32,72,128]{2,1,0:T(8,128)(2,1)S(1)}, u32[]{:S(2)}, u32[]{:S(2)}) collective-permute-start(bf16[32,72,128]{2,1,0:T(8,128)(2,1)S(1)} %bitcast.14), channel_id=1, source_target_pairs={{0,96},{1,33},{8,104},{9,41},{16,112},{17,49},{24,120},{25,57},{12... | collective-permute-start | bytes 1769480 | tf_op jit(solution)/shard_map/ppermute | solution.py:224
  32.3 12.2 %collective-permute-start.3 = (bf16[32,72,128]{2,1,0:T(8,128)(2,1)S(1)}, bf16[32,72,128]{2,1,0:T(8,128)(2,1)S(1)}, u32[]{:S(2)}, u32[]{:S(2)}) collective-permute-start(bf16[32,72,128]{2,1,0:T(8,128)(2,1)S(1)} %bitcast.15), channel_id=1, source_target_pairs={{0,6},{1,3},{8,14},{9,11},{16,22},{17,19},{24,30},{25,27},{128,134... | collective-permute-start | bytes 1769480 | tf_op jit(solution)/shard_map/ppermute | solution.py:224
  35.1 12.3 %collective-permute-start.2 = (bf16[32,72,128]{2,1,0:T(8,128)(2,1)S(1)}, bf16[32,72,128]{2,1,0:T(8,128)(2,1)S(1)}, u32[]{:S(2)}, u32[]{:S(2)}) collective-permute-start(bf16[32,72,128]{2,1,0:T(8,128)(2,1)S(1)} %bitcast.17), channel_id=1, source_target_pairs={{0,1},{1,0},{8,9},{9,8},{16,17},{17,16},{24,25},{25,24},{128,129},... | collective-permute-start | bytes 1769480 | tf_op jit(solution)/shard_map/ppermute | solution.py:227
  39.2 8.2 %collective-permute-start.8 = (bf16[32,72,128]{2,1,0:T(8,128)(2,1)S(1)}, bf16[32,72,128]{2,1,0:T(8,128)(2,1)S(1)}, u32[]{:S(2)}, u32[]{:S(2)}) collective-permute-start(bf16[32,72,128]{2,1,0:T(8,128)(2,1)S(1)} %collective-permute-done.7.a3), channel_id=1, source_target_pairs={{0,1},{1,0},{8,9},{9,8},{16,17},{17,16},{24,25},{25,24},{128,129},... | collective-permute-start | bytes 1769480 | tf_op jit(solution)/shard_map/ppermute | solution.py:227
  44.6 2.8 %collective-permute-start.6 = (bf16[32,72,128]{2,1,0:T(8,128)(2,1)S(1)}, bf16[32,72,128]{2,1,0:T(8,128)(2,1)S(1)}, u32[]{:S(2)}, u32[]{:S(2)}) collective-permute-start(bf16[32,72,128]{2,1,0:T(8,128)(2,1)S(1)} %collective-permute-done.5.a2), channel_id=1, source_target_pairs={{0,1},{1,0},{8,9},{9,8},{16,17},{17,16},{24,25},{25,24},{128,129},... | collective-permute-start | bytes 1769480 | tf_op jit(solution)/shard_map/ppermute | solution.py:227
  44.6 3.3 %collective-permute-start.4 = (bf16[32,72,128]{2,1,0:T(8,128)(2,1)S(1)}, bf16[32,72,128]{2,1,0:T(8,128)(2,1)S(1)}, u32[]{:S(2)}, u32[]{:S(2)}) collective-permute-start(bf16[32,72,128]{2,1,0:T(8,128)(2,1)S(1)} %collective-permute-done.3.a1), channel_id=1, source_target_pairs={{0,1},{1,0},{8,9},{9,8},{16,17},{17,16},{24,25},{25,24},{128,129},... | collective-permute-start | bytes 1769480 | tf_op jit(solution)/shard_map/ppermute | solution.py:227
